TPU v7x, 512 devices: a whole 4x8x8 slice. The times are simulated.
512 devices in a mesh: rows: 512 (over z, y, x, core).
Axes of the slice: x: 4, y: 8, z: 8, core: 2. Of those that a mesh axis runs over, the one named last changes fastest.
Arguments:
- slab: bfloat16 [131072, 4096], P('rows'), may hold values from -100 to 100
- sketch_matrix: bfloat16 [64, 4096], replicated, may hold values from -0.09375 to 0.09375
Outputs:
- q_basis: bfloat16 [64, 131072], P(None, 'rows')
- projection: float32 [64, 4096], replicated
- triangle: float32 [64, 64], replicated
- gram: float32 [64, 64], replicated
All inputs are finite; a program needn't handle non-finite values.
Results may differ from a plain program's by a relative error of at most 0.002.
Values sent between devices are 32-bit elements; how exact they have to be, the bound alone decides.
No kernel may reach another device: no remote copies, remote signals or barrier semaphores. Data moves between devices by JAX's collectives and lax.ppermute only.
A program may use at most 64 MiB of HBM per device.

v0:
```python
import math

import jax
import jax.numpy as jnp
from jax import lax
from jax.sharding import PartitionSpec as P


def symmetric_fold(cross_part, sketch_cols):
    folded = jnp.dot(
        cross_part,
        sketch_cols.astype(jnp.float32).T,
        precision=lax.Precision.HIGHEST,
        preferred_element_type=jnp.float32,
    )
    return 0.5 * (folded + folded.T)


def shards(slab, sketch_matrix):
    devices = lax.axis_size("rows")
    total = slab.shape[0] * devices
    columns = slab.shape[1]
    root = math.sqrt(total)
    sketch_t = lax.dot_general(
        sketch_matrix, slab, (((1,), (1,)), ((), ())), preferred_element_type=jnp.float32
    )
    sketch_low = sketch_t.astype(jnp.bfloat16)
    cross_part = jnp.dot(sketch_low, slab, preferred_element_type=jnp.float32)
    cross = lax.psum(cross_part, "rows")
    full_gram = symmetric_fold(cross, sketch_matrix)
    full_lower = jnp.linalg.cholesky(full_gram)
    lower = full_lower / root
    basis_t = lax.linalg.triangular_solve(lower, sketch_t, left_side=True, lower=True)
    q_basis = basis_t.astype(jnp.bfloat16)
    projection = lax.linalg.triangular_solve(lower, cross, left_side=True, lower=True) / root
    gram = (
        jnp.dot(
            projection,
            projection.T,
            precision=lax.Precision.HIGHEST,
            preferred_element_type=jnp.float32,
        )
        / columns
    )
    return (q_basis, projection, lower.T, gram)


def solution(mesh):
    return jax.shard_map(
        shards,
        mesh=mesh,
        in_specs=(P("rows", None), P()),
        out_specs=(P(None, "rows"), P(), P(), P()),
        check_vma=False,
    )
```

profile of v0, /device:TPU:1, one launch (start us, length us, event | category | flops | bytes accessed | tf_op | source)
XLA Modules:
  0.0 317.0 jit_solution(2125148359246117911)
XLA Ops:
  7.2 0.0 copy-start
  7.2 0.0 all-reduce.2.cloned.1.call-start
  7.2 1.5 copy-done
  8.8 1.8 fusion.7
  10.6 1.5 fusion.4
  12.0 0.0 all-reduce.2.cloned.1.call-update
  12.0 279.7 %all-reduce.2.cloned.1.call-done = f32[64,4096]{1,0:T(8,128)} async-done(((f32[64,4096]{1,0:T(8,128)}), f32[64,4096]{1,0:T(8,128)}) %all-reduce.2.cloned.1.call-update) | async-done | bytes 1048592 | tf_op jit(solution)/shard_map/psum | solution.py:29
  291.7 0.0 copy-start.2
  291.7 2.0 fusion.8
  293.8 0.1 copy.6
  293.9 5.8 %cholesky.16 = f32[64,64]{1,0:T(8,128)S(1)} custom-call(f32[64,64]{1,0:T(8,128)S(1)} %fusion.3), custom_call_target="Cholesky" | custom-call | tf_op jit(solution)/shard_map/jit(cholesky)/cholesky | solution.py:31
  299.8 0.6 compare_reduce_fusion
  300.4 0.7 fusion.6
  301.1 0.7 copy.7
  301.8 4.9 %custom-call.8 = f32[1,64,64]{1,2,0:T(8,128)S(1)} custom-call(f32[1,64,64]{2,1,0:T(8,128)S(1)} %get-tuple-element.9), custom_call_target="InvertDiagBlocksLowerTriangular" | custom-call | tf_op jit(solution)/shard_map/triangular_solve | solution.py:33
  306.7 0.9 convolution_convert_fusion
  307.6 0.0 copy-done.2
  307.6 1.0 convolution_multiply_fusion
  308.6 0.0 copy-start.1
  308.6 1.6 convolution_multiply_fusion.1
  310.2 0.0 copy-done.1
  (2 shorter events, 0.0 us)
Async XLA Ops:
  7.2 1.6 copy-start
  7.2 284.5 %all-reduce.2.cloned.1.call-start = ((), (), s32[]{:S(2)}) async-start(), calls=%async_computation | async-start | bytes 2097152 | tf_op jit(solution)/shard_map/psum | solution.py:29
  291.7 15.8 %copy-start.2 = (f32[64,4096]{1,0:T(8,128)S(1)}, f32[64,4096]{1,0:T(8,128)}, u32[]{:S(2)}) copy-start(f32[64,4096]{1,0:T(8,128)} %all-reduce.2.cloned.1.call-done) | copy-start | bytes 3145732
  308.6 1.6 copy-start.1
Sparse Core Ops, SparseCore 0:
  13.7 278.0 all-reduce.1
where the time goes:
time: 317 us
  waiting for transfers between devices  280 us (88%)
  between operations  14.1 us (4%)
  other arithmetic  12.1 us (4%)
  matrix products  8.81 us (3%)
    psum x1, waiting for transfers between devices, shards(): cross = lax.psum(cross_part, 'rows')  280 us
    another operation x3, other arithmetic, shards(): full_lower = jnp.linalg.cholesky(full_gram)  6.52 us
  transfers between devices with their start and end apart: 1, of which 1 were waited for; matrix products, arithmetic and copies ran while one was open for 0% of the time, Pallas kernels for 0%

commit v1 on v0

--- a/solution.py
+++ b/solution.py
@@ -4,6 +4,42 @@
 import jax.numpy as jnp
 from jax import lax
 from jax.sharding import PartitionSpec as P
+
+SIZES = dict(z=8, y=8, x=4, c=2)
+
+
+def groups(axes):
+    out = {}
+    for index in range(math.prod(SIZES.values())):
+        rest, coords = index, {}
+        for name in reversed(SIZES):
+            rest, coords[name] = divmod(rest, SIZES[name])
+        key = tuple(value for name, value in coords.items() if name not in axes)
+        out.setdefault(key, []).append(index)
+    return list(out.values())
+
+
+def exchange(pieces, axes):
+    return lax.all_to_all(pieces, "rows", 0, 0, axis_index_groups=groups(axes), tiled=True)
+
+
+def scatter_sum(tiles, axes):
+    count = math.prod(SIZES[a] for a in axes)
+    got = exchange(tiles, axes)
+    return got.reshape(count, tiles.shape[0] // count, 8, 128).sum(0)
+
+
+def spread(tiles, axes):
+    count = math.prod(SIZES[a] for a in axes)
+    return exchange(jnp.tile(tiles, (count, 1, 1)), axes)
+
+
+def all_reduce(tiles):
+    part = scatter_sum(tiles, "c")
+    part = scatter_sum(part, "yx")
+    size = part.shape[0]
+    part = spread(part, "z").reshape(-1, size, 8, 128).sum(0)
+    return spread(spread(part, "yx"), "c")
 
 
 def symmetric_fold(cross_part, sketch_cols):
@@ -20,13 +56,17 @@
     devices = lax.axis_size("rows")
     total = slab.shape[0] * devices
     columns = slab.shape[1]
+    rank = sketch_matrix.shape[0]
     root = math.sqrt(total)
     sketch_t = lax.dot_general(
         sketch_matrix, slab, (((1,), (1,)), ((), ())), preferred_element_type=jnp.float32
     )
     sketch_low = sketch_t.astype(jnp.bfloat16)
     cross_part = jnp.dot(sketch_low, slab, preferred_element_type=jnp.float32)
-    cross = lax.psum(cross_part, "rows")
+    blocks = columns // 128
+    tiles = cross_part.reshape(rank, blocks, 128).transpose(1, 0, 2).reshape(-1, 8, 128)
+    tiles = all_reduce(tiles)
+    cross = tiles.reshape(blocks, rank, 128).transpose(1, 0, 2).reshape(rank, columns)
     full_gram = symmetric_fold(cross, sketch_matrix)
     full_lower = jnp.linalg.cholesky(full_gram)
     lower = full_lower / root

time: 317 us -> 104 us (0.33)
  waiting for transfers between devices: 280 us -> 0 us
  blocking collectives: 0 us -> 77.8 us
  between operations: 14.1 us -> 0.71 us
    psum x1 -> x0, waiting for transfers between devices: 280 us -> none  [shards(): cross = lax.psum(cross_part, 'rows')]
    all_to_all x0 -> x5, blocking collectives: none -> 77.8 us  [exchange(): lax.all_to_all(pieces, 'rows', 0, 0, axis_index_groups=groups(axes), tile...]
  transfers between devices with their start and end apart: 1 -> 0, of which waited for: 1 -> 0; matrix products, arithmetic and copies ran while one was open for 0% -> 0% of each run, Pallas kernels for 0% -> 0%
where the time goes in v1:
time: 104 us; the launch traced here: 103 us
  blocking collectives  77.8 us (75%)
  other arithmetic  13 us (12%)
  matrix products  8.96 us (9%)
  local copies, waits for them, and re-layouts  2.61 us (3%)
    all_to_all x5, blocking collectives, exchange(): lax.all_to_all(pieces, 'rows', 0, 0, axis_index_groups=groups(axes), tile...  77.8 us
    another operation x3, other arithmetic, shards(): full_lower = jnp.linalg.cholesky(full_gram)  6.52 us
    another operation x1, other arithmetic, shards(): lax.linalg.triangular_solve(lower, sketch_t, left_side=True, lower=True)  4.9 us
    dot_general x1, matrix products, shards(): jnp.dot(projection, projection.T, precision=lax.Precision.HIGHEST, prefer...  3.17 us
    unnamed x5, local copies, waits for them, and re-layouts  2.29 us

profile of v1, /device:TPU:1, one launch (start us, length us, event | category | flops | bytes accessed | tf_op | source)
XLA Modules:
  0.0 103.1 jit_solution(4051036677397868691)
XLA Ops:
  0.6 0.0 copy-start
  0.6 1.6 %copy-done = bf16[256,4096]{1,0:T(8,128)(2,1)S(1)} copy-done((bf16[256,4096]{1,0:T(8,128)(2,1)S(1)}, bf16[256,4096]{1,0:T(8,128)(2,1)}, u32[]{:S(2)}) %copy-start) | copy-done | bytes 2097176
  2.2 1.8 %fusion.11 = f32[64,256]{1,0:T(8,128)S(1)} fusion(bf16[64,4096]{1,0:T(8,128)(2,1)} %param.3, bf16[256,4096]{1,0:T(8,128)(2,1)S(1)} %copy-done), kind=kOutput, calls=%fused_computation.23 | convolution fusion | flops 134217728 | bytes 2686976 | tf_op jit(solution)/shard_map/dot_general | solution.py:61
  4.0 0.5 convolution_bitcast_fusion
  4.5 0.1 copy.30
  4.6 11.1 %all_to_all.25 = f32[256,8,128]{2,1,0:T(8,128)S(1)} all-to-all(f32[256,8,128]{2,1,0:T(8,128)S(1)} %bitcast.47), channel_id=1, replica_groups={{0,1},{2,3},{4,5},{6,7},{8,9},{10,11},{12,13},{14,15},{16,17},{18,19},{..., dimensions={0} | all-to-all | bytes 2097152 | tf_op jit(solution)/shard_map/all_to_all | solution.py:23
  15.7 0.9 reduce_sum.27
  16.6 20.9 %all_to_all.26 = f32[128,8,128]{2,1,0:T(8,128)S(1)} all-to-all(f32[128,8,128]{2,1,0:T(8,128)} %reduce_sum.27), channel_id=1, replica_groups={{0,2,4,6,8,10,12,14,16,18,20,22,24,26,28,30,32,34,36,38,40,42,44,46,48,..., dimensions={0} | all-to-all | bytes 1048576 | tf_op jit(solution)/shard_map/all_to_all | solution.py:23
  37.6 17.9 %all_to_all.27 = f32[32,8,128]{2,1,0:T(8,128)S(1)} all-to-all(f32[32,8,128]{2,1,0:T(8,128)S(1)} %bitcast.53), channel_id=1, replica_groups={{0,64,128,192,256,320,384,448},{1,65,129,193,257,321,385,449},{2,66,130..., dimensions={0} | all-to-all | bytes 262144 | tf_op jit(solution)/shard_map/all_to_all | solution.py:23
  55.4 0.1 tile.14
  55.5 18.1 %all_to_all.28 = f32[128,8,128]{2,1,0:T(8,128)S(1)} all-to-all(f32[128,8,128]{2,1,0:T(8,128)S(1)} %bitcast.51), channel_id=1, replica_groups={{0,2,4,6,8,10,12,14,16,18,20,22,24,26,28,30,32,34,36,38,40,42,44,46,48,..., dimensions={0} | all-to-all | bytes 1048576 | tf_op jit(solution)/shard_map/all_to_all | solution.py:23
  73.6 0.0 copy-start.1
  73.6 0.1 tile.31
  73.7 9.9 %all_to_all.29 = f32[256,8,128]{2,1,0:T(8,128)S(1)} all-to-all(f32[256,8,128]{2,1,0:T(8,128)S(1)} %bitcast.49), channel_id=1, replica_groups={{0,1},{2,3},{4,5},{6,7},{8,9},{10,11},{12,13},{14,15},{16,17},{18,19},{..., dimensions={0} | all-to-all | bytes 2097152 | tf_op jit(solution)/shard_map/all_to_all | solution.py:23
  83.5 0.0 copy-done.1
  83.5 0.6 fusion.1
  84.1 0.1 copy.17
  84.2 5.8 %cholesky.16 = f32[64,64]{1,0:T(8,128)S(1)} custom-call(f32[64,64]{1,0:T(8,128)S(1)} %fusion.8), custom_call_target="Cholesky" | custom-call | tf_op jit(solution)/shard_map/jit(cholesky)/cholesky | solution.py:71
  90.1 0.6 compare_reduce_fusion
  90.8 0.7 fusion.10
  91.4 4.9 %custom-call.8 = f32[1,64,64]{1,2,0:T(8,128)S(1)} custom-call(f32[1,64,64]{2,1,0:T(8,128)S(1)} %get-tuple-element.21), custom_call_target="InvertDiagBlocksLowerTriangular" | custom-call | tf_op jit(solution)/shard_map/triangular_solve | solution.py:73
  96.3 0.9 convolution_convert_fusion
  97.2 2.0 %convolution_multiply_fusion = f32[64,4096]{1,0:T(8,128)} fusion(f32[32,8,8,128]{3,2,1,0:T(8,128)S(1)} %bitcast.46, f32[1,64,64]{1,2,0:T(8,128)S(1)} %custom-call.8), kind=kOutput, calls=%fused_computation | convolution fusion | flops 201588736 | bytes 2113536 | tf_op jit(solution)/shard_map/triangular_solve | solution.py:75
  99.2 0.7 copy.18
  99.9 3.2 %convolution_multiply_fusion.1 = f32[64,64]{1,0:T(8,128)} fusion(f32[64,4096]{1,0:T(8,128)} %convolution_multiply_fusion), kind=kOutput, calls=%fused_computation.3 | convolution fusion | flops 201330688 | bytes 1064960 | tf_op jit(solution)/shard_map/dot_general | solution.py:77
  (5 shorter events, 0.1 us)
Async XLA Ops:
  0.6 1.6 %copy-start = (bf16[256,4096]{1,0:T(8,128)(2,1)S(1)}, bf16[256,4096]{1,0:T(8,128)(2,1)}, u32[]{:S(2)}) copy-start(bf16[256,4096]{1,0:T(8,128)(2,1)} %param.2) | copy-start | bytes 6291460
  73.6 9.9 %copy-start.1 = (bf16[64,4096]{1,0:T(8,128)(2,1)S(1)}, bf16[64,4096]{1,0:T(8,128)(2,1)}, u32[]{:S(2)}) copy-start(bf16[64,4096]{1,0:T(8,128)(2,1)} %param.3) | copy-start | bytes 1572868

commit v2 on v0

--- a/solution.py
+++ b/solution.py
@@ -4,6 +4,56 @@
 import jax.numpy as jnp
 from jax import lax
 from jax.sharding import PartitionSpec as P
+
+SIZES = dict(z=8, y=8, x=4, c=2)
+
+
+def place(index):
+    coords = {}
+    for name in reversed(SIZES):
+        index, coords[name] = divmod(index, SIZES[name])
+    return coords
+
+
+def groups(axes_of_core):
+    out = {}
+    for index in range(math.prod(SIZES.values())):
+        coords = place(index)
+        axes = axes_of_core[coords["c"]]
+        key = (coords["c"],) + tuple(value for name, value in coords.items() if name not in axes)
+        out.setdefault(key, []).append(index)
+    return list(out.values())
+
+
+PLANE = groups(("yx", "zx"))
+LINE = groups(("z", "y"))
+PAIRS = [(i, i ^ 1) for i in range(math.prod(SIZES.values()))]
+
+
+def exchange(pieces, peers):
+    return lax.all_to_all(pieces, "rows", 0, 0, axis_index_groups=peers, tiled=True)
+
+
+def summed(tiles, count):
+    return tiles.reshape(count, tiles.shape[0] // count, 8, 128).sum(0)
+
+
+def spread(tiles, peers):
+    return exchange(jnp.tile(tiles, (len(peers[0]), 1, 1)), peers)
+
+
+def all_reduce(tiles):
+    core = lax.axis_index("rows") % 2
+    half = tiles.shape[0] // 2
+    give = lax.dynamic_slice_in_dim(tiles, (1 - core) * half, half)
+    keep = lax.dynamic_slice_in_dim(tiles, core * half, half)
+    part = keep + lax.ppermute(give, "rows", PAIRS)
+    part = summed(exchange(part, PLANE), len(PLANE[0]))
+    part = summed(spread(part, LINE), len(LINE[0]))
+    mine = spread(part, PLANE)
+    other = lax.ppermute(mine, "rows", PAIRS)
+    first = core == 0
+    return jnp.concatenate([jnp.where(first, mine, other), jnp.where(first, other, mine)], 0)
 
 
 def symmetric_fold(cross_part, sketch_cols):
@@ -20,13 +70,17 @@
     devices = lax.axis_size("rows")
     total = slab.shape[0] * devices
     columns = slab.shape[1]
+    rank = sketch_matrix.shape[0]
     root = math.sqrt(total)
     sketch_t = lax.dot_general(
         sketch_matrix, slab, (((1,), (1,)), ((), ())), preferred_element_type=jnp.float32
     )
     sketch_low = sketch_t.astype(jnp.bfloat16)
     cross_part = jnp.dot(sketch_low, slab, preferred_element_type=jnp.float32)
-    cross = lax.psum(cross_part, "rows")
+    blocks = columns // 128
+    tiles = cross_part.reshape(rank, blocks, 128).transpose(1, 0, 2).reshape(-1, 8, 128)
+    tiles = all_reduce(tiles)
+    cross = tiles.reshape(blocks, rank, 128).transpose(1, 0, 2).reshape(rank, columns)
     full_gram = symmetric_fold(cross, sketch_matrix)
     full_lower = jnp.linalg.cholesky(full_gram)
     lower = full_lower / root

time: 317 us -> 96.7 us (0.31)
  waiting for transfers between devices: 280 us -> 3.35 us
  blocking collectives: 0 us -> 51.4 us
  starting transfers between devices: 0.04 us -> 15 us
  between operations: 14.1 us -> 0.78 us
    psum x1 -> x0, waiting for transfers between devices: 280 us -> none  [shards(): cross = lax.psum(cross_part, 'rows')]
    all_to_all x0 -> x3, blocking collectives: none -> 51.4 us  [exchange(): lax.all_to_all(pieces, 'rows', 0, 0, axis_index_groups=peers, tiled=True)]
    ppermute x0 -> x2, starting transfers between devices: none -> 15 us  [the longest x1 8.78 us: all_reduce(): part = keep + lax.ppermute(give, 'rows', PAIRS)]
    ppermute x0 -> x2, waiting for transfers between devices: none -> 3.35 us  [the longest x1 1.85 us: all_reduce(): part = keep + lax.ppermute(give, 'rows', PAIRS)]
  transfers between devices with their start and end apart: 1 -> 2, of which waited for: 1 -> 2; matrix products, arithmetic and copies ran while one was open for 0% -> 0% of each run, Pallas kernels for 0% -> 0%
where the time goes in v2:
time: 96.7 us; the launch traced here: 96.3 us
  blocking collectives  51.4 us (53%)
  starting transfers between devices  15 us (16%)
  other arithmetic  13.4 us (14%)
  matrix products  8.96 us (9%)
  local copies, waits for them, and re-layouts  3.37 us (3%)
  waiting for transfers between devices  3.35 us (3%)
    all_to_all x3, blocking collectives, exchange(): lax.all_to_all(pieces, 'rows', 0, 0, axis_index_groups=peers, tiled=True)  51.4 us
    ppermute x1, starting transfers between devices, all_reduce(): part = keep + lax.ppermute(give, 'rows', PAIRS)  8.78 us
    another operation x3, other arithmetic, shards(): full_lower = jnp.linalg.cholesky(full_gram)  6.52 us
    ppermute x1, starting transfers between devices, all_reduce(): other = lax.ppermute(mine, 'rows', PAIRS)  6.23 us
    another operation x1, other arithmetic, shards(): lax.linalg.triangular_solve(lower, sketch_t, left_side=True, lower=True)  4.9 us
    dot_general x1, matrix products, shards(): jnp.dot(projection, projection.T, precision=lax.Precision.HIGHEST, prefer...  3.17 us
    unnamed x5, local copies, waits for them, and re-layouts  2.28 us
    another operation x1, matrix products, shards(): lax.linalg.triangular_solve(lower, cross, left_side=True, lower=True) / root  2.01 us
  transfers between devices with their start and end apart: 2, of which 2 were waited for; matrix products, arithmetic and copies ran while one was open for 0% of the time, Pallas kernels for 0%

profile of v2, /device:TPU:1, one launch (start us, length us, event | category | flops | bytes accessed | tf_op | source)
XLA Modules:
  0.0 96.3 jit_solution(9703877293909943655)
XLA Ops:
  0.6 0.0 copy-start
  0.7 1.6 %copy-done = bf16[256,4096]{1,0:T(8,128)(2,1)S(1)} copy-done((bf16[256,4096]{1,0:T(8,128)(2,1)S(1)}, bf16[256,4096]{1,0:T(8,128)(2,1)}, u32[]{:S(2)}) %copy-start) | copy-done | bytes 2097176
  2.2 1.8 %fusion.11 = f32[64,256]{1,0:T(8,128)S(1)} fusion(bf16[64,4096]{1,0:T(8,128)(2,1)} %param.3, bf16[256,4096]{1,0:T(8,128)(2,1)S(1)} %copy-done), kind=kOutput, calls=%fused_computation.28 | convolution fusion | flops 134217728 | bytes 2686976 | tf_op jit(solution)/shard_map/dot_general | solution.py:75
  4.0 0.5 convolution_bitcast_fusion
  4.5 0.1 copy.30
  4.6 0.8 constant_dynamic-slice_fusion
  5.5 8.8 %collective-permute-start = (f32[128,8,128]{2,1,0:T(8,128)}, f32[128,8,128]{2,1,0:T(8,128)}, u32[]{:S(2)}, u32[]{:S(2)}) collective-permute-start(f32[128,8,128]{2,1,0:T(8,128)} %constant_dynamic-slice_fusion), channel_id=1, source_target_pairs={{0,1},{1,0},{2,3},{3,2},{4,5},{5,4},{6,7},{7,6},{8,9},{9,8},{10,11... | collective-permute-start | bytes 1572872 | tf_op jit(solution)/shard_map/ppermute | solution.py:50
  14.3 1.8 %collective-permute-done = f32[128,8,128]{2,1,0:T(8,128)} collective-permute-done((f32[128,8,128]{2,1,0:T(8,128)}, f32[128,8,128]{2,1,0:T(8,128)}, u32[]{:S(2)}, u32[]{:S(2)}) %collective-permute-start) | collective-permute-done | bytes 524320 | tf_op jit(solution)/shard_map/ppermute | solution.py:50
  16.1 1.1 %dynamic-slice_add_fusion = f32[128,8,128]{2,1,0:T(8,128)S(1)} fusion(f32[128,8,128]{2,1,0:T(8,128)} %collective-permute-done, f32[256,8,128]{2,1,0:T(8,128)S(1)} %bitcast.46, s32[]{:T(128)S(6)} %select_n.31), kind=kLoop, calls=%fused_computation.11 | loop fusion | flops 131072 | bytes 1572868 | tf_op jit(solution)/shard_map/add | solution.py:50
  17.2 20.0 %all_to_all.15 = f32[128,8,128]{2,1,0:T(8,128)S(1)} all-to-all(f32[128,8,128]{2,1,0:T(8,128)S(1)} %dynamic-slice_add_fusion), channel_id=1, replica_groups={{0,2,4,6,8,10,12,14,16,18,20,22,24,26,28,30,32,34,36,38,40,42,44,46,48,..., dimensions={0} | all-to-all | bytes 1048576 | tf_op jit(solution)/shard_map/all_to_all | solution.py:34
  37.3 14.5 %all_to_all.16 = f32[32,8,128]{2,1,0:T(8,128)S(1)} all-to-all(f32[32,8,128]{2,1,0:T(8,128)S(1)} %bitcast.50), channel_id=1, replica_groups={{0,64,128,192,256,320,384,448},{1,9,17,25,33,41,49,57},{2,66,130,194,25..., dimensions={0} | all-to-all | bytes 262144 | tf_op jit(solution)/shard_map/all_to_all | solution.py:34
  51.8 0.1 tile.20
  51.9 16.9 %all_to_all.17 = f32[128,8,128]{2,1,0:T(8,128)S(1)} all-to-all(f32[128,8,128]{2,1,0:T(8,128)S(1)} %bitcast.48), channel_id=1, replica_groups={{0,2,4,6,8,10,12,14,16,18,20,22,24,26,28,30,32,34,36,38,40,42,44,46,48,..., dimensions={0} | all-to-all | bytes 1048576 | tf_op jit(solution)/shard_map/all_to_all | solution.py:34
  68.8 6.2 %collective-permute-start.1 = (f32[128,8,128]{2,1,0:T(8,128)S(1)}, f32[128,8,128]{2,1,0:T(8,128)S(1)}, u32[]{:S(2)}, u32[]{:S(2)}) collective-permute-start(f32[128,8,128]{2,1,0:T(8,128)S(1)} %all_to_all.17), channel_id=1, source_target_pairs={{0,1},{1,0},{2,3},{3,2},{4,5},{5,4},{6,7},{7,6},{8,9},{9,8},{10,11... | collective-permute-start | bytes 1572872 | tf_op jit(solution)/shard_map/ppermute | solution.py:54
  75.0 0.0 copy-start.1
  75.1 1.5 %collective-permute-done.1 = f32[128,8,128]{2,1,0:T(8,128)S(1)} collective-permute-done((f32[128,8,128]{2,1,0:T(8,128)S(1)}, f32[128,8,128]{2,1,0:T(8,128)S(1)}, u32[]{:S(2)}, u32[]{:S(2)}) %collective-permute-start.1) | collective-permute-done | bytes 524320 | tf_op jit(solution)/shard_map/ppermute | solution.py:54
  76.5 0.1 broadcast_select_fusion.1
  76.6 0.1 pad_maximum_fusion
  76.7 0.0 copy-done.1
  76.7 0.6 fusion.1
  77.3 0.1 copy.17
  77.4 5.8 %cholesky.16 = f32[64,64]{1,0:T(8,128)S(1)} custom-call(f32[64,64]{1,0:T(8,128)S(1)} %fusion.8), custom_call_target="Cholesky" | custom-call | tf_op jit(solution)/shard_map/jit(cholesky)/cholesky | solution.py:85
  83.3 0.6 compare_reduce_fusion
  84.0 0.7 fusion.10
  84.6 4.9 %custom-call.8 = f32[1,64,64]{1,2,0:T(8,128)S(1)} custom-call(f32[1,64,64]{2,1,0:T(8,128)S(1)} %get-tuple-element.23), custom_call_target="InvertDiagBlocksLowerTriangular" | custom-call | tf_op jit(solution)/shard_map/triangular_solve | solution.py:87
  89.5 0.9 convolution_convert_fusion
  90.4 2.0 %convolution_multiply_fusion = f32[64,4096]{1,0:T(8,128)} fusion(f32[32,8,8,128]{3,2,1,0:T(8,128)S(1)} %bitcast.44, f32[1,64,64]{1,2,0:T(8,128)S(1)} %custom-call.8), kind=kOutput, calls=%fused_computation | convolution fusion | flops 201588736 | bytes 2113536 | tf_op jit(solution)/shard_map/triangular_solve | solution.py:89
  92.4 0.7 copy.18
  93.1 3.2 %convolution_multiply_fusion.1 = f32[64,64]{1,0:T(8,128)} fusion(f32[64,4096]{1,0:T(8,128)} %convolution_multiply_fusion), kind=kOutput, calls=%fused_computation.3 | convolution fusion | flops 201330688 | bytes 1064960 | tf_op jit(solution)/shard_map/dot_general | solution.py:91
  (5 shorter events, 0.1 us)
Async XLA Ops:
  0.6 1.6 %copy-start = (bf16[256,4096]{1,0:T(8,128)(2,1)S(1)}, bf16[256,4096]{1,0:T(8,128)(2,1)}, u32[]{:S(2)}) copy-start(bf16[256,4096]{1,0:T(8,128)(2,1)} %param.2) | copy-start | bytes 6291460
  5.5 10.6 %collective-permute-start = (f32[128,8,128]{2,1,0:T(8,128)}, f32[128,8,128]{2,1,0:T(8,128)}, u32[]{:S(2)}, u32[]{:S(2)}) collective-permute-start(f32[128,8,128]{2,1,0:T(8,128)} %constant_dynamic-slice_fusion), channel_id=1, source_target_pairs={{0,1},{1,0},{2,3},{3,2},{4,5},{5,4},{6,7},{7,6},{8,9},{9,8},{10,11... | collective-permute-start | bytes 1572872 | tf_op jit(solution)/shard_map/ppermute | solution.py:50
  68.8 7.8 %collective-permute-start.1 = (f32[128,8,128]{2,1,0:T(8,128)S(1)}, f32[128,8,128]{2,1,0:T(8,128)S(1)}, u32[]{:S(2)}, u32[]{:S(2)}) collective-permute-start(f32[128,8,128]{2,1,0:T(8,128)S(1)} %all_to_all.17), channel_id=1, source_target_pairs={{0,1},{1,0},{2,3},{3,2},{4,5},{5,4},{6,7},{7,6},{8,9},{9,8},{10,11... | collective-permute-start | bytes 1572872 | tf_op jit(solution)/shard_map/ppermute | solution.py:54
  75.0 1.7 %copy-start.1 = (bf16[64,4096]{1,0:T(8,128)(2,1)S(1)}, bf16[64,4096]{1,0:T(8,128)(2,1)}, u32[]{:S(2)}) copy-start(bf16[64,4096]{1,0:T(8,128)(2,1)} %param.3) | copy-start | bytes 1572868

commit v3 on v2

v3 whole, which is shorter than its diff:
```python
import functools
import math

import jax
import jax.numpy as jnp
from jax import lax
from jax.experimental import pallas as pl
from jax.experimental.pallas import tpu as pltpu
from jax.sharding import PartitionSpec as P

SIZES = dict(z=8, y=8, x=4, c=2)


def place(index):
    coords = {}
    for name in reversed(SIZES):
        index, coords[name] = divmod(index, SIZES[name])
    return coords


def groups(axes_of_core):
    out = {}
    for index in range(math.prod(SIZES.values())):
        coords = place(index)
        axes = axes_of_core[coords["c"]]
        key = (coords["c"],) + tuple(value for name, value in coords.items() if name not in axes)
        out.setdefault(key, []).append(index)
    return list(out.values())


PLANE = groups(("yx", "zx"))
LINE = groups(("z", "y"))
PAIRS = [(i, i ^ 1) for i in range(math.prod(SIZES.values()))]


def exchange(pieces, peers):
    return lax.all_to_all(pieces, "rows", 0, 0, axis_index_groups=peers, tiled=True)


def summed(tiles, count):
    return tiles.reshape(count, tiles.shape[0] // count, 8, 128).sum(0)


def spread(tiles, peers):
    return exchange(jnp.tile(tiles, (len(peers[0]), 1, 1)), peers)


def all_reduce(tiles, core):
    half = tiles.shape[0] // 2
    give = lax.dynamic_slice_in_dim(tiles, (1 - core) * half, half)
    keep = lax.dynamic_slice_in_dim(tiles, core * half, half)
    part = keep + lax.ppermute(give, "rows", PAIRS)
    part = summed(exchange(part, PLANE), len(PLANE[0]))
    part = summed(spread(part, LINE), len(LINE[0]))
    mine = spread(part, PLANE)
    return mine, lax.ppermute(mine, "rows", PAIRS)


LAST = (((1,), (1,)), ((), ()))


def split(value, parts):
    out = []
    for _ in range(parts):
        out.append(value.astype(jnp.bfloat16))
        value = value - out[-1].astype(jnp.float32)
    return out


def eliminate(work, size):
    sub = lax.broadcasted_iota(jnp.int32, (8, 128), 0)

    def row(tile, k):
        return jnp.broadcast_to(tile[k : k + 1, :], (8, 128))

    work = [work[8 * b : 8 * b + 8] for b in range(work.shape[0] // 8)]
    for first in range(0, 8 * len(work), size):
        top, at = divmod(first, 8)
        live = range(top, len(work))
        column = [
            {b: jnp.broadcast_to(work[b][:, first + k : first + k + 1], (8, 128)) for b in live}
            for k in range(size)
        ]
        pivot = [row(work[top], at + k) for k in range(size)]
        m = {(i, k): row(column[k][top], at + i) for k in range(size) for i in range(k, size)}
        x, done, scaled = {}, {}, {}
        for k in range(0, size, 2):
            a, b, d = m[k, k], m[k + 1, k], m[k + 1, k + 1]
            inverse = 1.0 / (a * d - b * b)
            ai, bi, di = a * inverse, b * inverse, d * inverse
            rest = range(k + 2, size)
            for i in rest:
                x[i, k] = di * m[i, k] - bi * m[i, k + 1]
                x[i, k + 1] = ai * m[i, k + 1] - bi * m[i, k]
            for i in rest:
                for j in range(k + 2, i + 1):
                    m[i, j] = m[i, j] - x[i, k] * m[j, k] - x[i, k + 1] * m[j, k + 1]
            done[k] = pivot[k]
            done[k + 1] = pivot[k + 1] - (b * (1.0 / a)) * pivot[k]
            scaled[k] = di * pivot[k] - bi * pivot[k + 1]
            scaled[k + 1] = ai * pivot[k + 1] - bi * pivot[k]
            for i in rest:
                pivot[i] = pivot[i] - x[i, k] * pivot[k] - x[i, k + 1] * pivot[k + 1]
        for k in reversed(range(size)):
            for i in range(k // 2 * 2 + 2, size):
                scaled[k] = scaled[k] - x[i, k] * scaled[i]
        for b in live:
            new = work[b]
            if b > top or at + size < 8:
                terms = [column[k][b] * scaled[k] for k in range(size)]
                while len(terms) > 1:
                    terms = [terms[i] + terms[i + 1] for i in range(0, len(terms), 2)]
                new = new - terms[0]
            if b == top:
                new = jnp.where(sub >= at + size, new, work[b])
                for k in range(1, size):
                    new = jnp.where(sub == at + k, done[k], new)
            work[b] = new
    return jnp.concatenate(work, 0)


def factor(gram):
    n = gram.shape[0]
    row = lax.broadcasted_iota(jnp.int32, (n, n), 0)
    col = lax.broadcasted_iota(jnp.int32, (n, n), 1)
    on_diag = jnp.where(row == col, gram, 0.0)
    diag_row = jnp.sum(on_diag, 0, keepdims=True)
    down = lax.rsqrt(jnp.sum(on_diag, 1, keepdims=True))
    across = lax.rsqrt(diag_row)
    scale = jnp.where(row == col, jnp.broadcast_to(down, (n, n)), 0.0)
    work = eliminate(jnp.concatenate([gram * down * across, scale], 1), 8)
    upper = work[:, :n]
    left = lax.rsqrt(jnp.sum(jnp.where(row == col, upper, 0.0), 1, keepdims=True))
    return jnp.where(col >= row, upper * left * (diag_row * across), 0.0), work[:, n:] * left


def post(root, core_ref, mine_ref, other_ref, sketch_ref, sketch_t_ref, q_ref, proj_ref, tri_ref, gram_ref, stack):
    rank, columns = proj_ref.shape
    half = columns // 2
    blocks = half // 128
    core = core_ref[0]
    places = [pl.ds(pl.multiple_of(c * half, half), half) for c in (core, 1 - core)]
    folded = jnp.zeros((3 * rank, rank), jnp.float32)
    for i, source in enumerate((mine_ref, other_ref)):
        cross = jnp.concatenate([source[b] for b in range(blocks)], 1)
        high, mid, low = split(cross, 3)
        three = jnp.concatenate([high, mid, low], 0)
        stack[i, : 3 * rank] = three
        stack[i, 3 * rank :] = high
        folded += lax.dot_general(three, sketch_ref[:, places[i]], LAST, preferred_element_type=jnp.float32)
    folded = folded[:rank] + (folded[rank : 2 * rank] + folded[2 * rank :])
    upper, inverse = factor(0.5 * (folded + folded.T))
    tri_ref[...] = upper * (1.0 / root)
    high, low = split(inverse, 2)
    left = jnp.concatenate([high, high, high, low], 1)
    total = jnp.zeros((2 * rank, rank), jnp.float32)
    for i in range(2):
        part = jnp.dot(left, stack[i], preferred_element_type=jnp.float32)
        proj_ref[:, places[i]] = part
        pair = split(part, 2)
        total += lax.dot_general(
            jnp.concatenate(pair, 0), pair[0], LAST, preferred_element_type=jnp.float32
        )
    gram_ref[...] = (total[:rank] + (total[rank:] + total[rank:].T)) * (1.0 / columns)
    high, low = split(inverse * root, 2)
    left = jnp.concatenate([high, high, low], 1)
    s_high, s_low = split(sketch_t_ref[...], 2)
    right = jnp.concatenate([s_high, s_low, s_high], 0)
    q_ref[...] = jnp.dot(left, right, preferred_element_type=jnp.float32).astype(q_ref.dtype)


def finish(core, mine, other, sketch_matrix, sketch_t, root):
    rank, columns = sketch_matrix.shape
    vmem = pl.BlockSpec(memory_space=pltpu.VMEM)
    return pl.pallas_call(
        functools.partial(post, root),
        out_shape=(
            jax.ShapeDtypeStruct(sketch_t.shape, jnp.bfloat16),
            jax.ShapeDtypeStruct((rank, columns), jnp.float32),
            jax.ShapeDtypeStruct((rank, rank), jnp.float32),
            jax.ShapeDtypeStruct((rank, rank), jnp.float32),
        ),
        in_specs=[pl.BlockSpec(memory_space=pltpu.SMEM)] + [vmem] * 4,
        out_specs=[vmem] * 4,
        scratch_shapes=[pltpu.VMEM((2, 4 * rank, columns // 2), jnp.bfloat16)],
        compiler_params=pltpu.CompilerParams(vmem_limit_bytes=24 << 20),
        name="factor_and_project",
    )(core, mine, other, sketch_matrix, sketch_t)


def shards(slab, sketch_matrix):
    devices = lax.axis_size("rows")
    core = lax.axis_index("rows") % 2
    rank, columns = sketch_matrix.shape
    sketch_t = lax.dot_general(sketch_matrix, slab, LAST, preferred_element_type=jnp.float32)
    sketch_low = sketch_t.astype(jnp.bfloat16)
    cross_part = jnp.dot(sketch_low, slab, preferred_element_type=jnp.float32)
    blocks = columns // 128
    tiles = cross_part.reshape(rank, blocks, 128).transpose(1, 0, 2).reshape(-1, 8, 128)
    halves = [half.reshape(blocks // 2, rank, 128) for half in all_reduce(tiles, core)]
    return finish(core.reshape(1), *halves, sketch_matrix, sketch_t, math.sqrt(slab.shape[0] * devices))


def solution(mesh):
    return jax.shard_map(
        shards,
        mesh=mesh,
        in_specs=(P("rows", None), P()),
        out_specs=(P(None, "rows"), P(), P(), P()),
        check_vma=False,
    )
```

time: 96.7 us -> 82.5 us (0.85)
  other arithmetic: 13.4 us -> 1.15 us
  matrix products: 8.96 us -> 2.28 us
  Pallas kernels: 0 us -> 5.39 us
    another operation x4 -> x0, other arithmetic: 11.4 us -> none  [the longest x3 6.52 us: shards(): full_lower = jnp.linalg.cholesky(full_gram)]
    pallas_call x0 -> x1, Pallas kernels: none -> 5.39 us  [finish(): pl.pallas_call(functools.partial(post, root), out_shape=(jax.ShapeDtypeSt...]
    dot_general x3 -> x1, matrix products: 5.58 us -> 1.8 us  [shards(): lax.dot_general(sketch_matrix, slab, LAST, preferred_element_type=jnp.flo...]
    another operation x2 -> x0, matrix products: 2.89 us -> none  [the longest x1 2.01 us: shards(): lax.linalg.triangular_solve(lower, cross, left_side=True, lower=True) / root]
    unnamed x5 -> x4, local copies, waits for them, and re-layouts: 2.28 us -> 1.58 us
where the time goes in v3:
time: 82.5 us; the launch traced here: 82.1 us
  blocking collectives  51.6 us (63%)
  starting transfers between devices  15 us (18%)
  Pallas kernels  5.39 us (7%)
  waiting for transfers between devices  3.36 us (4%)
  local copies, waits for them, and re-layouts  2.6 us (3%)
  matrix products  2.28 us (3%)
  other arithmetic  1.15 us (1%)
    all_to_all x3, blocking collectives, exchange(): lax.all_to_all(pieces, 'rows', 0, 0, axis_index_groups=peers, tiled=True)  51.6 us
    ppermute x1, starting transfers between devices, all_reduce(): part = keep + lax.ppermute(give, 'rows', PAIRS)  8.78 us
    ppermute x1, starting transfers between devices, all_reduce(): return (mine, lax.ppermute(mine, 'rows', PAIRS))  6.23 us
    pallas_call x1, Pallas kernels, finish(): pl.pallas_call(functools.partial(post, root), out_shape=(jax.ShapeDtypeSt...  5.39 us
    ppermute x1, waiting for transfers between devices, all_reduce(): part = keep + lax.ppermute(give, 'rows', PAIRS)  1.85 us
    dot_general x1, matrix products, shards(): lax.dot_general(sketch_matrix, slab, LAST, preferred_element_type=jnp.flo...  1.8 us
  transfers between devices with their start and end apart: 2, of which 2 were waited for; matrix products, arithmetic and copies ran while one was open for 0% of the time, Pallas kernels for 0%

profile of v3, /device:TPU:1, one launch (start us, length us, event | category | flops | bytes accessed | tf_op | source)
XLA Modules:
  0.0 82.1 jit_solution(10548372689581472485)
XLA Ops:
  0.6 0.0 copy-start
  0.7 1.6 %copy-done = bf16[256,4096]{1,0:T(8,128)(2,1)S(1)} copy-done((bf16[256,4096]{1,0:T(8,128)(2,1)S(1)}, bf16[256,4096]{1,0:T(8,128)(2,1)}, u32[]{:S(2)}) %copy-start) | copy-done | bytes 2097176
  2.2 1.8 %fusion.1.sketch_t_ref = f32[64,256]{1,0:T(8,128)S(1)} fusion(bf16[64,4096]{1,0:T(8,128)(2,1)} %sketch_ref.1, bf16[256,4096]{1,0:T(8,128)(2,1)S(1)} %copy-done), kind=kOutput, calls=%fused_computation.5 | convolution fusion | flops 134217728 | bytes 2686976 | tf_op jit(solution)/shard_map/dot_general | solution.py:195
  4.0 0.5 convolution_bitcast_fusion
  4.5 0.1 copy.10
  4.6 0.8 %constant_dynamic-slice_fusion = f32[128,8,128]{2,1,0:T(8,128)} fusion(f32[256,8,128]{2,1,0:T(8,128)S(1)} %bitcast.20, s32[]{:T(128)S(6)} %select_n.15), kind=kLoop, calls=%fused_computation.4 | loop fusion | bytes 1048580 | tf_op jit(solution)/shard_map/dynamic_slice | solution.py:50
  5.5 8.8 %collective-permute-start = (f32[128,8,128]{2,1,0:T(8,128)}, f32[128,8,128]{2,1,0:T(8,128)}, u32[]{:S(2)}, u32[]{:S(2)}) collective-permute-start(f32[128,8,128]{2,1,0:T(8,128)} %constant_dynamic-slice_fusion), channel_id=1, source_target_pairs={{0,1},{1,0},{2,3},{3,2},{4,5},{5,4},{6,7},{7,6},{8,9},{9,8},{10,11... | collective-permute-start | bytes 1572872 | tf_op jit(solution)/shard_map/ppermute | solution.py:52
  14.3 1.8 %collective-permute-done = f32[128,8,128]{2,1,0:T(8,128)} collective-permute-done((f32[128,8,128]{2,1,0:T(8,128)}, f32[128,8,128]{2,1,0:T(8,128)}, u32[]{:S(2)}, u32[]{:S(2)}) %collective-permute-start) | collective-permute-done | bytes 524320 | tf_op jit(solution)/shard_map/ppermute | solution.py:52
  16.1 1.1 %dynamic-slice_add_fusion = f32[128,8,128]{2,1,0:T(8,128)S(1)} fusion(f32[128,8,128]{2,1,0:T(8,128)} %collective-permute-done, f32[256,8,128]{2,1,0:T(8,128)S(1)} %bitcast.21, s32[]{:T(128)S(6)} %select_n.14), kind=kLoop, calls=%fused_computation.2 | loop fusion | flops 131072 | bytes 1572868 | tf_op jit(solution)/shard_map/add | solution.py:52
  17.2 0.0 copy-start.1
  17.2 20.1 %all_to_all.15 = f32[128,8,128]{2,1,0:T(8,128)S(1)} all-to-all(f32[128,8,128]{2,1,0:T(8,128)S(1)} %dynamic-slice_add_fusion), channel_id=1, replica_groups={{0,2,4,6,8,10,12,14,16,18,20,22,24,26,28,30,32,34,36,38,40,42,44,46,48,..., dimensions={0} | all-to-all | bytes 1048576 | tf_op jit(solution)/shard_map/all_to_all | solution.py:37
  37.4 14.5 %all_to_all.16 = f32[32,8,128]{2,1,0:T(8,128)S(1)} all-to-all(f32[32,8,128]{2,1,0:T(8,128)S(1)} %bitcast.25), channel_id=1, replica_groups={{0,64,128,192,256,320,384,448},{1,9,17,25,33,41,49,57},{2,66,130,194,25..., dimensions={0} | all-to-all | bytes 262144 | tf_op jit(solution)/shard_map/all_to_all | solution.py:37
  52.0 0.1 tile.20
  52.0 16.9 %all_to_all.17 = f32[128,8,128]{2,1,0:T(8,128)S(1)} all-to-all(f32[128,8,128]{2,1,0:T(8,128)S(1)} %bitcast.23), channel_id=1, replica_groups={{0,2,4,6,8,10,12,14,16,18,20,22,24,26,28,30,32,34,36,38,40,42,44,46,48,..., dimensions={0} | all-to-all | bytes 1048576 | tf_op jit(solution)/shard_map/all_to_all | solution.py:37
  68.9 6.2 %collective-permute-start.1 = (f32[128,8,128]{2,1,0:T(8,128)S(1)}, f32[128,8,128]{2,1,0:T(8,128)S(1)}, u32[]{:S(2)}, u32[]{:S(2)}) collective-permute-start(f32[128,8,128]{2,1,0:T(8,128)S(1)} %all_to_all.17), channel_id=1, source_target_pairs={{0,1},{1,0},{2,3},{3,2},{4,5},{5,4},{6,7},{7,6},{8,9},{9,8},{10,11... | collective-permute-start | bytes 1572872 | tf_op jit(solution)/shard_map/ppermute | solution.py:56
  75.2 1.5 %collective-permute-done.1 = f32[128,8,128]{2,1,0:T(8,128)S(1)} collective-permute-done((f32[128,8,128]{2,1,0:T(8,128)S(1)}, f32[128,8,128]{2,1,0:T(8,128)S(1)}, u32[]{:S(2)}, u32[]{:S(2)}) %collective-permute-start.1) | collective-permute-done | bytes 524320 | tf_op jit(solution)/shard_map/ppermute | solution.py:56
  76.7 0.0 copy-done.1
  76.7 5.4 %factor_and_project.1 = (bf16[64,256]{1,0:T(8,128)(2,1)}, f32[64,4096]{1,0:T(8,128)}, f32[64,64]{1,0:T(8,128)}, f32[64,64]{1,0:T(8,128)}) custom-call(s32[1]{0:T(128)} %bitcast.core_ref, f32[16,64,128]{2,1,0:T(8,128)S(1)} %bitcast.18, f32[16,64,128]{2,1,0:T(8,128)S(1)} %bitcast.19, bf16[64,4096]{1,0:T(8,128)(2,1)S(1)} %copy-done.1, ...), custom_call_target="tpu_custom_call" | custom-call | tf_op jit(solution)/shard_map/factor_and_project/pallas_call | solution.py:175
  (3 shorter events, 0.1 us)
Async XLA Ops:
  0.6 1.6 %copy-start = (bf16[256,4096]{1,0:T(8,128)(2,1)S(1)}, bf16[256,4096]{1,0:T(8,128)(2,1)}, u32[]{:S(2)}) copy-start(bf16[256,4096]{1,0:T(8,128)(2,1)} %param.2) | copy-start | bytes 6291460
  5.5 10.6 %collective-permute-start = (f32[128,8,128]{2,1,0:T(8,128)}, f32[128,8,128]{2,1,0:T(8,128)}, u32[]{:S(2)}, u32[]{:S(2)}) collective-permute-start(f32[128,8,128]{2,1,0:T(8,128)} %constant_dynamic-slice_fusion), channel_id=1, source_target_pairs={{0,1},{1,0},{2,3},{3,2},{4,5},{5,4},{6,7},{7,6},{8,9},{9,8},{10,11... | collective-permute-start | bytes 1572872 | tf_op jit(solution)/shard_map/ppermute | solution.py:52
  17.2 59.5 %copy-start.1 = (bf16[64,4096]{1,0:T(8,128)(2,1)S(1)}, bf16[64,4096]{1,0:T(8,128)(2,1)}, u32[]{:S(2)}) copy-start(bf16[64,4096]{1,0:T(8,128)(2,1)} %sketch_ref.1) | copy-start | bytes 1572868
  68.9 7.8 %collective-permute-start.1 = (f32[128,8,128]{2,1,0:T(8,128)S(1)}, f32[128,8,128]{2,1,0:T(8,128)S(1)}, u32[]{:S(2)}, u32[]{:S(2)}) collective-permute-start(f32[128,8,128]{2,1,0:T(8,128)S(1)} %all_to_all.17), channel_id=1, source_target_pairs={{0,1},{1,0},{2,3},{3,2},{4,5},{5,4},{6,7},{7,6},{8,9},{9,8},{10,11... | collective-permute-start | bytes 1572872 | tf_op jit(solution)/shard_map/ppermute | solution.py:56

commit v4 on v3

--- a/solution.py
+++ b/solution.py
@@ -45,10 +45,7 @@
     return exchange(jnp.tile(tiles, (len(peers[0]), 1, 1)), peers)
 
 
-def all_reduce(tiles, core):
-    half = tiles.shape[0] // 2
-    give = lax.dynamic_slice_in_dim(tiles, (1 - core) * half, half)
-    keep = lax.dynamic_slice_in_dim(tiles, core * half, half)
+def all_reduce(give, keep):
     part = keep + lax.ppermute(give, "rows", PAIRS)
     part = summed(exchange(part, PLANE), len(PLANE[0]))
     part = summed(spread(part, LINE), len(LINE[0]))
@@ -134,6 +131,61 @@
     return jnp.where(col >= row, upper * left * (diag_row * across), 0.0), work[:, n:] * left
 
 
+def pre(core_ref, slab_hbm, sketch_hbm, sketch_t_ref, give_ref, keep_ref, slab_ref, sketch_ref, arrived):
+    columns = slab_ref.shape[1]
+    chunks = arrived.shape[1]
+    width = columns // chunks
+    views = [pl.ds(i * width, width) for i in range(chunks)]
+    copies = [
+        [
+            pltpu.make_async_copy(source.at[:, view], target.at[:, view], arrived.at[j, i])
+            for j, (source, target) in enumerate(((sketch_hbm, sketch_ref), (slab_hbm, slab_ref)))
+        ]
+        for i, view in enumerate(views)
+    ]
+    for pair in copies:
+        for copy in pair:
+            copy.start()
+    sketch_t = jnp.zeros(sketch_t_ref.shape, jnp.float32)
+    for pair, view in zip(copies, views):
+        for copy in pair:
+            copy.wait()
+        sketch_t += lax.dot_general(
+            sketch_ref[:, view], slab_ref[:, view], LAST, preferred_element_type=jnp.float32
+        )
+    sketch_t_ref[...] = sketch_t
+    sketch_low = sketch_t.astype(jnp.bfloat16)
+    core = core_ref[0]
+    half = columns // 2
+    for c, out_ref in ((1 - core, give_ref), (core, keep_ref)):
+        view = pl.ds(pl.multiple_of(c * half, half), half)
+        part = jnp.dot(sketch_low, slab_ref[:, view], preferred_element_type=jnp.float32)
+        for b in range(half // 128):
+            out_ref[b] = part[:, b * 128 : (b + 1) * 128]
+
+
+def begin(core, slab, sketch_matrix, chunks=4):
+    rows, columns = slab.shape
+    rank = sketch_matrix.shape[0]
+    vmem = pl.BlockSpec(memory_space=pltpu.VMEM)
+    hbm = pl.BlockSpec(memory_space=pltpu.HBM)
+    slab, sketch_matrix = (pltpu.with_memory_space_constraint(a, pltpu.HBM) for a in (slab, sketch_matrix))
+    half = pltpu.VMEM((columns // 256, rank, 128), jnp.float32)
+    return pl.pallas_call(
+        pre,
+        out_shape=(pltpu.VMEM((rank, rows), jnp.float32), half, half),
+        in_specs=[pl.BlockSpec(memory_space=pltpu.SMEM), hbm, hbm],
+        out_specs=[vmem] * 3,
+        scratch_shapes=[
+            pltpu.VMEM(slab.shape, slab.dtype),
+            pltpu.VMEM(sketch_matrix.shape, sketch_matrix.dtype),
+            pltpu.SemaphoreType.DMA((2, chunks)),
+        ],
+        compiler_params=pltpu.CompilerParams(vmem_limit_bytes=16 << 20),
+        name="sketch_and_cross",
+    )(core, slab, sketch_matrix)
+
+
 def post(root, core_ref, mine_ref, other_ref, sketch_ref, sketch_t_ref, q_ref, proj_ref, tri_ref, gram_ref, stack):
     rank, columns = proj_ref.shape
     half = columns // 2
@@ -190,15 +242,12 @@
 
 def shards(slab, sketch_matrix):
     devices = lax.axis_size("rows")
-    core = lax.axis_index("rows") % 2
-    rank, columns = sketch_matrix.shape
-    sketch_t = lax.dot_general(sketch_matrix, slab, LAST, preferred_element_type=jnp.float32)
-    sketch_low = sketch_t.astype(jnp.bfloat16)
-    cross_part = jnp.dot(sketch_low, slab, preferred_element_type=jnp.float32)
-    blocks = columns // 128
-    tiles = cross_part.reshape(rank, blocks, 128).transpose(1, 0, 2).reshape(-1, 8, 128)
-    halves = [half.reshape(blocks // 2, rank, 128) for half in all_reduce(tiles, core)]
-    return finish(core.reshape(1), *halves, sketch_matrix, sketch_t, math.sqrt(slab.shape[0] * devices))
+    core = (lax.axis_index("rows") % 2).reshape(1)
+    sketch_t, give, keep = begin(core, slab, sketch_matrix)
+    shape = give.shape
+    halves = all_reduce(give.reshape(-1, 8, 128), keep.reshape(-1, 8, 128))
+    mine, other = (half.reshape(shape) for half in halves)
+    return finish(core, mine, other, sketch_matrix, sketch_t, math.sqrt(slab.shape[0] * devices))
 
 
 def solution(mesh):

time: 82.5 us -> 79.4 us (0.962)
  Pallas kernels: 5.39 us -> 8.59 us
  local copies, waits for them, and re-layouts: 2.6 us -> 0.07 us
  matrix products: 2.28 us -> 0 us
  other arithmetic: 1.15 us -> 0.11 us
    pallas_call x0 -> x1, Pallas kernels: none -> 3.19 us  [begin(): pl.pallas_call(pre, out_shape=(pltpu.VMEM((rank, rows), jnp.float32), hal...]
    dot_general x2 -> x0, matrix products: 2.28 us -> none  [the longest x1 1.8 us: shards(): lax.dot_general(sketch_matrix, slab, LAST, preferred_element_type=jnp.flo...]
    unnamed x4 -> x2, local copies, waits for them, and re-layouts: 1.58 us -> 0.01 us
    add x1, other arithmetic: 1.1 us -> 0.05 us  [all_reduce(): part = keep + lax.ppermute(give, 'rows', PAIRS)]
    dynamic_slice x1 -> x0, local copies, waits for them, and re-layouts: 0.83 us -> none  [all_reduce(): give = lax.dynamic_slice_in_dim(tiles, (1 - core) * half, half)]
where the time goes in v4:
time: 79.4 us; the launch traced here: 79.1 us
  blocking collectives  51.6 us (65%)
  starting transfers between devices  15 us (19%)
  Pallas kernels  8.59 us (11%)
  waiting for transfers between devices  3.03 us (4%)
    all_to_all x3, blocking collectives, exchange(): lax.all_to_all(pieces, 'rows', 0, 0, axis_index_groups=peers, tiled=True)  51.6 us
    ppermute x1, starting transfers between devices, all_reduce(): part = keep + lax.ppermute(give, 'rows', PAIRS)  8.79 us
    ppermute x1, starting transfers between devices, all_reduce(): return (mine, lax.ppermute(mine, 'rows', PAIRS))  6.23 us
    pallas_call x1, Pallas kernels, finish(): pl.pallas_call(functools.partial(post, root), out_shape=(jax.ShapeDtypeSt...  5.4 us
    pallas_call x1, Pallas kernels, begin(): pl.pallas_call(pre, out_shape=(pltpu.VMEM((rank, rows), jnp.float32), hal...  3.19 us
  transfers between devices with their start and end apart: 2, of which 2 were waited for; matrix products, arithmetic and copies ran while one was open for 0% of the time, Pallas kernels for 0%

profile of v4, /device:TPU:1, one launch (start us, length us, event | category | flops | bytes accessed | tf_op | source)
XLA Modules:
  0.0 79.1 jit_solution(13412824553149065846)
XLA Ops:
  0.6 3.2 %sketch_and_cross.1 = (f32[64,256]{1,0:T(8,128)S(1)}, f32[16,64,128]{2,1,0:T(8,128)S(1)}, f32[16,64,128]{2,1,0:T(8,128)S(1)}) custom-call(s32[1]{0:T(128)} %bitcast.core_ref, bf16[256,4096]{1,0:T(8,128)(2,1)} %slab_hbm.1, bf16[64,4096]{1,0:T(8,128)(2,1)} %sketch_ref.1), custom_call_target="tpu_custom_call" | custom-call | tf_op jit(solution)/shard_map/sketch_and_cross/pallas_call | solution.py:174
  3.8 8.8 %collective-permute-start = (f32[128,8,128]{2,1,0:T(8,128)S(1)}, f32[128,8,128]{2,1,0:T(8,128)S(1)}, u32[]{:S(2)}, u32[]{:S(2)}) collective-permute-start(f32[128,8,128]{2,1,0:T(8,128)S(1)} %bitcast.12), channel_id=1, source_target_pairs={{0,1},{1,0},{2,3},{3,2},{4,5},{5,4},{6,7},{7,6},{8,9},{9,8},{10,11... | collective-permute-start | bytes 1572872 | tf_op jit(solution)/shard_map/ppermute | solution.py:49
  12.6 1.5 %collective-permute-done = f32[128,8,128]{2,1,0:T(8,128)S(1)} collective-permute-done((f32[128,8,128]{2,1,0:T(8,128)S(1)}, f32[128,8,128]{2,1,0:T(8,128)S(1)}, u32[]{:S(2)}, u32[]{:S(2)}) %collective-permute-start) | collective-permute-done | bytes 524320 | tf_op jit(solution)/shard_map/ppermute | solution.py:49
  14.2 0.1 add.8
  14.2 0.0 copy-start
  14.2 20.1 %all_to_all.15 = f32[128,8,128]{2,1,0:T(8,128)S(1)} all-to-all(f32[128,8,128]{2,1,0:T(8,128)S(1)} %add.8), channel_id=1, replica_groups={{0,2,4,6,8,10,12,14,16,18,20,22,24,26,28,30,32,34,36,38,40,42,44,46,48,..., dimensions={0} | all-to-all | bytes 1048576 | tf_op jit(solution)/shard_map/all_to_all | solution.py:37
  34.4 14.6 %all_to_all.16 = f32[32,8,128]{2,1,0:T(8,128)S(1)} all-to-all(f32[32,8,128]{2,1,0:T(8,128)S(1)} %bitcast.16), channel_id=1, replica_groups={{0,64,128,192,256,320,384,448},{1,9,17,25,33,41,49,57},{2,66,130,194,25..., dimensions={0} | all-to-all | bytes 262144 | tf_op jit(solution)/shard_map/all_to_all | solution.py:37
  49.0 0.1 tile.20
  49.0 16.9 %all_to_all.17 = f32[128,8,128]{2,1,0:T(8,128)S(1)} all-to-all(f32[128,8,128]{2,1,0:T(8,128)S(1)} %bitcast.14), channel_id=1, replica_groups={{0,2,4,6,8,10,12,14,16,18,20,22,24,26,28,30,32,34,36,38,40,42,44,46,48,..., dimensions={0} | all-to-all | bytes 1048576 | tf_op jit(solution)/shard_map/all_to_all | solution.py:37
  65.9 6.2 %collective-permute-start.1 = (f32[128,8,128]{2,1,0:T(8,128)S(1)}, f32[128,8,128]{2,1,0:T(8,128)S(1)}, u32[]{:S(2)}, u32[]{:S(2)}) collective-permute-start(f32[128,8,128]{2,1,0:T(8,128)S(1)} %all_to_all.17), channel_id=1, source_target_pairs={{0,1},{1,0},{2,3},{3,2},{4,5},{5,4},{6,7},{7,6},{8,9},{9,8},{10,11... | collective-permute-start | bytes 1572872 | tf_op jit(solution)/shard_map/ppermute | solution.py:53
  72.2 1.5 %collective-permute-done.1 = f32[128,8,128]{2,1,0:T(8,128)S(1)} collective-permute-done((f32[128,8,128]{2,1,0:T(8,128)S(1)}, f32[128,8,128]{2,1,0:T(8,128)S(1)}, u32[]{:S(2)}, u32[]{:S(2)}) %collective-permute-start.1) | collective-permute-done | bytes 524320 | tf_op jit(solution)/shard_map/ppermute | solution.py:53
  73.7 0.0 copy-done
  73.7 5.4 %factor_and_project.1 = (bf16[64,256]{1,0:T(8,128)(2,1)}, f32[64,4096]{1,0:T(8,128)}, f32[64,64]{1,0:T(8,128)}, f32[64,64]{1,0:T(8,128)}) custom-call(s32[1]{0:T(128)} %bitcast.core_ref, f32[16,64,128]{2,1,0:T(8,128)S(1)} %bitcast.9, f32[16,64,128]{2,1,0:T(8,128)S(1)} %bitcast.11, bf16[64,4096]{1,0:T(8,128)(2,1)S(1)} %copy-done, ...), custom_call_target="tpu_custom_call" | custom-call | tf_op jit(solution)/shard_map/factor_and_project/pallas_call | solution.py:227
  (3 shorter events, 0.1 us)
Async XLA Ops:
  3.8 10.3 %collective-permute-start = (f32[128,8,128]{2,1,0:T(8,128)S(1)}, f32[128,8,128]{2,1,0:T(8,128)S(1)}, u32[]{:S(2)}, u32[]{:S(2)}) collective-permute-start(f32[128,8,128]{2,1,0:T(8,128)S(1)} %bitcast.12), channel_id=1, source_target_pairs={{0,1},{1,0},{2,3},{3,2},{4,5},{5,4},{6,7},{7,6},{8,9},{9,8},{10,11... | collective-permute-start | bytes 1572872 | tf_op jit(solution)/shard_map/ppermute | solution.py:49
  14.2 59.5 %copy-start = (bf16[64,4096]{1,0:T(8,128)(2,1)S(1)}, bf16[64,4096]{1,0:T(8,128)(2,1)}, u32[]{:S(2)}) copy-start(bf16[64,4096]{1,0:T(8,128)(2,1)} %sketch_ref.1) | copy-start | bytes 1572868
  65.9 7.8 %collective-permute-start.1 = (f32[128,8,128]{2,1,0:T(8,128)S(1)}, f32[128,8,128]{2,1,0:T(8,128)S(1)}, u32[]{:S(2)}, u32[]{:S(2)}) collective-permute-start(f32[128,8,128]{2,1,0:T(8,128)S(1)} %all_to_all.17), channel_id=1, source_target_pairs={{0,1},{1,0},{2,3},{3,2},{4,5},{5,4},{6,7},{7,6},{8,9},{9,8},{10,11... | collective-permute-start | bytes 1572872 | tf_op jit(solution)/shard_map/ppermute | solution.py:53

commit v5 on v4

--- a/solution.py
+++ b/solution.py
@@ -45,12 +45,10 @@
     return exchange(jnp.tile(tiles, (len(peers[0]), 1, 1)), peers)
 
 
-def all_reduce(give, keep):
-    part = keep + lax.ppermute(give, "rows", PAIRS)
+def all_reduce(part):
     part = summed(exchange(part, PLANE), len(PLANE[0]))
     part = summed(spread(part, LINE), len(LINE[0]))
-    mine = spread(part, PLANE)
-    return mine, lax.ppermute(mine, "rows", PAIRS)
+    return spread(part, PLANE)
 
 
 LAST = (((1,), (1,)), ((), ()))
@@ -131,7 +129,7 @@
     return jnp.where(col >= row, upper * left * (diag_row * across), 0.0), work[:, n:] * left
 
 
-def pre(core_ref, slab_hbm, sketch_hbm, sketch_t_ref, give_ref, keep_ref, slab_ref, sketch_ref, arrived):
+def pre(core_ref, slab_hbm, sketch_hbm, sketch_t_ref, slab_ref, give_ref, sketch_ref, arrived):
     columns = slab_ref.shape[1]
     chunks = arrived.shape[1]
     width = columns // chunks
@@ -154,61 +152,111 @@
             sketch_ref[:, view], slab_ref[:, view], LAST, preferred_element_type=jnp.float32
         )
     sketch_t_ref[...] = sketch_t
-    sketch_low = sketch_t.astype(jnp.bfloat16)
-    core = core_ref[0]
-    half = columns // 2
-    for c, out_ref in ((1 - core, give_ref), (core, keep_ref)):
-        view = pl.ds(pl.multiple_of(c * half, half), half)
-        part = jnp.dot(sketch_low, slab_ref[:, view], preferred_element_type=jnp.float32)
-        for b in range(half // 128):
-            out_ref[b] = part[:, b * 128 : (b + 1) * 128]
+    cross_half(1 - core_ref[0], sketch_t, slab_ref, give_ref)
+
+
+def cross_half(which, sketch_t, slab_ref, out_ref):
+    half = slab_ref.shape[1] // 2
+    view = pl.ds(pl.multiple_of(which * half, half), half)
+    part = jnp.dot(sketch_t.astype(jnp.bfloat16), slab_ref[:, view], preferred_element_type=jnp.float32)
+    for b in range(half // 128):
+        out_ref[b] = part[:, b * 128 : (b + 1) * 128]
+
+
+def pre_keep(core_ref, sketch_t_ref, slab_ref, keep_ref):
+    cross_half(core_ref[0], sketch_t_ref[...], slab_ref, keep_ref)
+
+
+SCALAR = pl.BlockSpec(memory_space=pltpu.SMEM)
+VMEM = pl.BlockSpec(memory_space=pltpu.VMEM)
+LIMIT = pltpu.CompilerParams(vmem_limit_bytes=16 << 20)
 
 
 def begin(core, slab, sketch_matrix, chunks=4):
     rows, columns = slab.shape
     rank = sketch_matrix.shape[0]
-    vmem = pl.BlockSpec(memory_space=pltpu.VMEM)
+    slab, sketch_matrix = (pltpu.with_memory_space_constraint(a, pltpu.HBM) for a in (slab, sketch_matrix))
     hbm = pl.BlockSpec(memory_space=pltpu.HBM)
-    slab, sketch_matrix = (pltpu.with_memory_space_constraint(a, pltpu.HBM) for a in (slab, sketch_matrix))
-    half = pltpu.VMEM((columns // 256, rank, 128), jnp.float32)
     return pl.pallas_call(
         pre,
-        out_shape=(pltpu.VMEM((rank, rows), jnp.float32), half, half),
-        in_specs=[pl.BlockSpec(memory_space=pltpu.SMEM), hbm, hbm],
-        out_specs=[vmem] * 3,
+        out_shape=(
+            pltpu.VMEM((rank, rows), jnp.float32),
+            pltpu.VMEM(slab.shape, slab.dtype),
+            pltpu.VMEM((columns // 256, rank, 128), jnp.float32),
+        ),
+        in_specs=[SCALAR, hbm, hbm],
+        out_specs=[VMEM] * 3,
         scratch_shapes=[
-            pltpu.VMEM(slab.shape, slab.dtype),
             pltpu.VMEM(sketch_matrix.shape, sketch_matrix.dtype),
             pltpu.SemaphoreType.DMA((2, chunks)),
         ],
-        compiler_params=pltpu.CompilerParams(vmem_limit_bytes=16 << 20),
-        name="sketch_and_cross",
+        compiler_params=LIMIT,
+        name="sketch_and_cross_to_give",
     )(core, slab, sketch_matrix)
 
 
-def post(root, core_ref, mine_ref, other_ref, sketch_ref, sketch_t_ref, q_ref, proj_ref, tri_ref, gram_ref, stack):
+def keep_half(core, sketch_t, slab):
+    rows, columns = slab.shape
+    rank = sketch_t.shape[0]
+    return pl.pallas_call(
+        pre_keep,
+        out_shape=pltpu.VMEM((columns // 256, rank, 128), jnp.float32),
+        in_specs=[SCALAR, VMEM, VMEM],
+        out_specs=VMEM,
+        compiler_params=LIMIT,
+        cost_estimate=pl.CostEstimate(flops=rank * rows * columns, bytes_accessed=slab.size, transcendentals=0),
+        name="cross_to_keep",
+    )(core, sketch_t, slab)
+
+
+def fold_half(which, source, sketch_ref, stack):
+    rank = sketch_ref.shape[0]
+    half = source.shape[0] * 128
+    cross = jnp.concatenate([source[b] for b in range(source.shape[0])], 1)
+    high, mid, low = split(cross, 3)
+    stack[...] = jnp.concatenate([high, mid, low, high], 0)
+    view = pl.ds(pl.multiple_of(which * half, half), half)
+    out = lax.dot_general(stack[: 3 * rank], sketch_ref[:, view], LAST, preferred_element_type=jnp.float32)
+    return out[:rank] + (out[rank : 2 * rank] + out[2 * rank :])
+
+
+def post_mine(core_ref, mine_ref, sketch_ref, stack, folded_ref):
+    folded_ref[...] = fold_half(core_ref[0], mine_ref, sketch_ref, stack)
+
+
+def fold_mine(core, mine, sketch_matrix):
+    rank, columns = sketch_matrix.shape
+    return pl.pallas_call(
+        post_mine,
+        out_shape=(
+            pltpu.VMEM((4 * rank, columns // 2), jnp.bfloat16),
+            pltpu.VMEM((rank, rank), jnp.float32),
+        ),
+        in_specs=[SCALAR, VMEM, VMEM],
+        out_specs=[VMEM] * 2,
+        compiler_params=LIMIT,
+        cost_estimate=pl.CostEstimate(
+            flops=3 * rank * rank * columns, bytes_accessed=4 * rank * columns, transcendentals=0
+        ),
+        name="fold_mine",
+    )(core, mine, sketch_matrix)
+
+
+def post(
+    root, core_ref, mine_stack, folded_ref, other_ref, sketch_ref, sketch_t_ref, q_ref, proj_ref, tri_ref, gram_ref, other_stack
+):
     rank, columns = proj_ref.shape
     half = columns // 2
-    blocks = half // 128
     core = core_ref[0]
-    places = [pl.ds(pl.multiple_of(c * half, half), half) for c in (core, 1 - core)]
-    folded = jnp.zeros((3 * rank, rank), jnp.float32)
-    for i, source in enumerate((mine_ref, other_ref)):
-        cross = jnp.concatenate([source[b] for b in range(blocks)], 1)
-        high, mid, low = split(cross, 3)
-        three = jnp.concatenate([high, mid, low], 0)
-        stack[i, : 3 * rank] = three
-        stack[i, 3 * rank :] = high
-        folded += lax.dot_general(three, sketch_ref[:, places[i]], LAST, preferred_element_type=jnp.float32)
-    folded = folded[:rank] + (folded[rank : 2 * rank] + folded[2 * rank :])
+    folded = folded_ref[...] + fold_half(1 - core, other_ref, sketch_ref, other_stack)
     upper, inverse = factor(0.5 * (folded + folded.T))
     tri_ref[...] = upper * (1.0 / root)
     high, low = split(inverse, 2)
     left = jnp.concatenate([high, high, high, low], 1)
     total = jnp.zeros((2 * rank, rank), jnp.float32)
-    for i in range(2):
-        part = jnp.dot(left, stack[i], preferred_element_type=jnp.float32)
-        proj_ref[:, places[i]] = part
+    for which, stack in ((core, mine_stack), (1 - core, other_stack)):
+        part = jnp.dot(left, stack[...], preferred_element_type=jnp.float32)
+        proj_ref[:, pl.ds(pl.multiple_of(which * half, half), half)] = part
         pair = split(part, 2)
         total += lax.dot_general(
             jnp.concatenate(pair, 0), pair[0], LAST, preferred_element_type=jnp.float32
@@ -221,9 +269,8 @@
     q_ref[...] = jnp.dot(left, right, preferred_element_type=jnp.float32).astype(q_ref.dtype)
 
 
-def finish(core, mine, other, sketch_matrix, sketch_t, root):
+def finish(core, mine_stack, folded, other, sketch_matrix, sketch_t, root):
     rank, columns = sketch_matrix.shape
-    vmem = pl.BlockSpec(memory_space=pltpu.VMEM)
     return pl.pallas_call(
         functools.partial(post, root),
         out_shape=(
@@ -232,22 +279,25 @@
             jax.ShapeDtypeStruct((rank, rank), jnp.float32),
             jax.ShapeDtypeStruct((rank, rank), jnp.float32),
         ),
-        in_specs=[pl.BlockSpec(memory_space=pltpu.SMEM)] + [vmem] * 4,
-        out_specs=[vmem] * 4,
-        scratch_shapes=[pltpu.VMEM((2, 4 * rank, columns // 2), jnp.bfloat16)],
+        in_specs=[SCALAR] + [VMEM] * 5,
+        out_specs=[VMEM] * 4,
+        scratch_shapes=[pltpu.VMEM((4 * rank, columns // 2), jnp.bfloat16)],
         compiler_params=pltpu.CompilerParams(vmem_limit_bytes=24 << 20),
         name="factor_and_project",
-    )(core, mine, other, sketch_matrix, sketch_t)
+    )(core, mine_stack, folded, other, sketch_matrix, sketch_t)
 
 
 def shards(slab, sketch_matrix):
     devices = lax.axis_size("rows")
     core = (lax.axis_index("rows") % 2).reshape(1)
-    sketch_t, give, keep = begin(core, slab, sketch_matrix)
+    sketch_t, slab_near, give = begin(core, slab, sketch_matrix)
     shape = give.shape
-    halves = all_reduce(give.reshape(-1, 8, 128), keep.reshape(-1, 8, 128))
-    mine, other = (half.reshape(shape) for half in halves)
-    return finish(core, mine, other, sketch_matrix, sketch_t, math.sqrt(slab.shape[0] * devices))
+    got = lax.ppermute(give, "rows", PAIRS)
+    keep = keep_half(core, sketch_t, slab_near)
+    mine = all_reduce((keep + got).reshape(-1, 8, 128)).reshape(shape)
+    other = lax.ppermute(mine, "rows", PAIRS)
+    stack, folded = fold_mine(core, mine, sketch_matrix)
+    return finish(core, stack, folded, other, sketch_matrix, sketch_t, math.sqrt(slab.shape[0] * devices))
 
 
 def solution(mesh):

time: 79.4 us -> 78.7 us (level)
    pallas_call x1 -> x3, Pallas kernels: 3.19 us -> 3.74 us  [the longest x1 3.01 us: begin(): pl.pallas_call(pre, out_shape=(pltpu.VMEM((rank, rows), jnp.float32), plt...]
  transfers between devices with their start and end apart: 2 -> 2, of which waited for: 2 -> 2; matrix products, arithmetic and copies ran while one was open for 0% -> 0% of each run, Pallas kernels for 0% -> 1%
where the time goes in v5:
time: 78.7 us; the launch traced here: 78.4 us
  blocking collectives  51.6 us (66%)
  starting transfers between devices  15 us (19%)
  Pallas kernels  8.64 us (11%)
  waiting for transfers between devices  2.29 us (3%)
    all_to_all x3, blocking collectives, exchange(): lax.all_to_all(pieces, 'rows', 0, 0, axis_index_groups=peers, tiled=True)  51.6 us
    ppermute x1, starting transfers between devices, shards(): got = lax.ppermute(give, 'rows', PAIRS)  8.79 us
    ppermute x1, starting transfers between devices, shards(): other = lax.ppermute(mine, 'rows', PAIRS)  6.23 us
    pallas_call x1, Pallas kernels, finish(): pl.pallas_call(functools.partial(post, root), out_shape=(jax.ShapeDtypeSt...  4.9 us
    pallas_call x1, Pallas kernels, begin(): pl.pallas_call(pre, out_shape=(pltpu.VMEM((rank, rows), jnp.float32), plt...  3.01 us
  transfers between devices with their start and end apart: 2, of which 2 were waited for; matrix products, arithmetic and copies ran while one was open for 0% of the time, Pallas kernels for 1%

profile of v5, /device:TPU:1, one launch (start us, length us, event | category | flops | bytes accessed | tf_op | source)
XLA Modules:
  0.0 78.4 jit_solution(1900712151679511749)
XLA Ops:
  0.6 3.0 %sketch_and_cross_to_give.1 = (f32[64,256]{1,0:T(8,128)S(1)}, bf16[256,4096]{1,0:T(8,128)(2,1)S(1)}, f32[16,64,128]{2,1,0:T(8,128)S(1)}) custom-call(s32[1]{0:T(128)} %bitcast.core_ref, bf16[256,4096]{1,0:T(8,128)(2,1)} %slab_hbm.1, bf16[64,4096]{1,0:T(8,128)(2,1)} %sketch_ref.3), custom_call_target="tpu_custom_call" | custom-call | tf_op jit(solution)/shard_map/sketch_and_cross_to_give/pallas_call | solution.py:180
  3.7 8.8 %collective-permute-start = (f32[16,64,128]{2,1,0:T(8,128)S(1)}, f32[16,64,128]{2,1,0:T(8,128)S(1)}, u32[]{:S(2)}, u32[]{:S(2)}) collective-permute-start(f32[16,64,128]{2,1,0:T(8,128)S(1)} %get-tuple-element.11), channel_id=1, source_target_pairs={{0,1},{1,0},{2,3},{3,2},{4,5},{5,4},{6,7},{7,6},{8,9},{9,8},{10,11... | collective-permute-start | bytes 1572872 | tf_op jit(solution)/shard_map/ppermute | solution.py:295
  12.5 0.3 cross_to_keep.1
  12.8 1.2 %collective-permute-done = f32[16,64,128]{2,1,0:T(8,128)S(1)} collective-permute-done((f32[16,64,128]{2,1,0:T(8,128)S(1)}, f32[16,64,128]{2,1,0:T(8,128)S(1)}, u32[]{:S(2)}, u32[]{:S(2)}) %collective-permute-start) | collective-permute-done | bytes 524320 | tf_op jit(solution)/shard_map/ppermute | solution.py:295
  14.0 0.1 add.8
  14.0 0.0 copy-start
  14.0 20.1 %all_to_all.15 = f32[128,8,128]{2,1,0:T(8,128)S(1)} all-to-all(f32[128,8,128]{2,1,0:T(8,128)S(1)} %bitcast.9), channel_id=1, replica_groups={{0,2,4,6,8,10,12,14,16,18,20,22,24,26,28,30,32,34,36,38,40,42,44,46,48,..., dimensions={0} | all-to-all | bytes 1048576 | tf_op jit(solution)/shard_map/all_to_all | solution.py:37
  34.2 14.5 %all_to_all.16 = f32[32,8,128]{2,1,0:T(8,128)S(1)} all-to-all(f32[32,8,128]{2,1,0:T(8,128)S(1)} %bitcast.13), channel_id=1, replica_groups={{0,64,128,192,256,320,384,448},{1,9,17,25,33,41,49,57},{2,66,130,194,25..., dimensions={0} | all-to-all | bytes 262144 | tf_op jit(solution)/shard_map/all_to_all | solution.py:37
  48.8 0.1 tile.20
  48.9 16.9 %all_to_all.17 = f32[128,8,128]{2,1,0:T(8,128)S(1)} all-to-all(f32[128,8,128]{2,1,0:T(8,128)S(1)} %bitcast.11), channel_id=1, replica_groups={{0,2,4,6,8,10,12,14,16,18,20,22,24,26,28,30,32,34,36,38,40,42,44,46,48,..., dimensions={0} | all-to-all | bytes 1048576 | tf_op jit(solution)/shard_map/all_to_all | solution.py:37
  65.8 6.2 %collective-permute-start.1 = (f32[16,64,128]{2,1,0:T(8,128)S(1)}, f32[16,64,128]{2,1,0:T(8,128)S(1)}, u32[]{:S(2)}, u32[]{:S(2)}) collective-permute-start(f32[16,64,128]{2,1,0:T(8,128)S(1)} %bitcast.7), channel_id=1, source_target_pairs={{0,1},{1,0},{2,3},{3,2},{4,5},{5,4},{6,7},{7,6},{8,9},{9,8},{10,11... | collective-permute-start | bytes 1572872 | tf_op jit(solution)/shard_map/ppermute | solution.py:298
  72.0 0.0 copy-done
  72.0 0.4 fold_mine.1
  72.4 1.1 %collective-permute-done.1.other_ref = f32[16,64,128]{2,1,0:T(8,128)S(1)} collective-permute-done((f32[16,64,128]{2,1,0:T(8,128)S(1)}, f32[16,64,128]{2,1,0:T(8,128)S(1)}, u32[]{:S(2)}, u32[]{:S(2)}) %collective-permute-start.1) | collective-permute-done | bytes 524320 | tf_op jit(solution)/shard_map/ppermute | solution.py:298
  73.5 4.9 %factor_and_project.1 = (bf16[64,256]{1,0:T(8,128)(2,1)}, f32[64,4096]{1,0:T(8,128)}, f32[64,64]{1,0:T(8,128)}, f32[64,64]{1,0:T(8,128)}) custom-call(s32[1]{0:T(128)} %bitcast.core_ref, bf16[256,2048]{1,0:T(8,128)(2,1)S(1)} %get-tuple-element.12.mine_stack, f32[64,64]{1,0:T(8,128)S(1)} %get-tuple-element.13.folded_ref, ...), custom_call_target="tpu_custom_call" | custom-call | tf_op jit(solution)/shard_map/factor_and_project/pallas_call | solution.py:274
  (3 shorter events, 0.1 us)
Async XLA Ops:
  3.7 10.3 %collective-permute-start = (f32[16,64,128]{2,1,0:T(8,128)S(1)}, f32[16,64,128]{2,1,0:T(8,128)S(1)}, u32[]{:S(2)}, u32[]{:S(2)}) collective-permute-start(f32[16,64,128]{2,1,0:T(8,128)S(1)} %get-tuple-element.11), channel_id=1, source_target_pairs={{0,1},{1,0},{2,3},{3,2},{4,5},{5,4},{6,7},{7,6},{8,9},{9,8},{10,11... | collective-permute-start | bytes 1572872 | tf_op jit(solution)/shard_map/ppermute | solution.py:295
  14.0 58.0 %copy-start = (bf16[64,4096]{1,0:T(8,128)(2,1)S(1)}, bf16[64,4096]{1,0:T(8,128)(2,1)}, u32[]{:S(2)}) copy-start(bf16[64,4096]{1,0:T(8,128)(2,1)} %sketch_ref.3) | copy-start | bytes 1572868
  65.8 7.8 %collective-permute-start.1 = (f32[16,64,128]{2,1,0:T(8,128)S(1)}, f32[16,64,128]{2,1,0:T(8,128)S(1)}, u32[]{:S(2)}, u32[]{:S(2)}) collective-permute-start(f32[16,64,128]{2,1,0:T(8,128)S(1)} %bitcast.7), channel_id=1, source_target_pairs={{0,1},{1,0},{2,3},{3,2},{4,5},{5,4},{6,7},{7,6},{8,9},{9,8},{10,11... | collective-permute-start | bytes 1572872 | tf_op jit(solution)/shard_map/ppermute | solution.py:298

commit v6 on v5

--- a/solution.py
+++ b/solution.py
@@ -62,7 +62,7 @@
     return out
 
 
-def eliminate(work, size):
+def eliminate(work, size, base):
     sub = lax.broadcasted_iota(jnp.int32, (8, 128), 0)
 
     def row(tile, k):
@@ -73,7 +73,7 @@
         top, at = divmod(first, 8)
         live = range(top, len(work))
         column = [
-            {b: jnp.broadcast_to(work[b][:, first + k : first + k + 1], (8, 128)) for b in live}
+            {b: jnp.broadcast_to(work[b][:, base + first + k : base + first + k + 1], (8, 128)) for b in live}
             for k in range(size)
         ]
         pivot = [row(work[top], at + k) for k in range(size)]
@@ -81,8 +81,18 @@
         x, done, scaled = {}, {}, {}
         for k in range(0, size, 2):
             a, b, d = m[k, k], m[k + 1, k], m[k + 1, k + 1]
-            inverse = 1.0 / (a * d - b * b)
-            ai, bi, di = a * inverse, b * inverse, d * inverse
+            if k % 4 == 0:
+                det = a * d - b * b
+                y = {i: (d * m[i, k] - b * m[i, k + 1], a * m[i, k + 1] - b * m[i, k]) for i in (k + 2, k + 3)}
+                e, f, g = (
+                    det * m[i, j] - (y[i][0] * m[j, k] + y[i][1] * m[j, k + 1])
+                    for i, j in ((k + 2, k + 2), (k + 3, k + 2), (k + 3, k + 3))
+                )
+                after = det * (1.0 / (e * g - f * f))
+                inverse = 1.0 / det
+                ai, bi, di = a * inverse, b * inverse, d * inverse
+            else:
+                ai, bi, di = e * after, f * after, g * after
             rest = range(k + 2, size)
             for i in rest:
                 x[i, k] = di * m[i, k] - bi * m[i, k + 1]
@@ -123,17 +133,28 @@
     down = lax.rsqrt(jnp.sum(on_diag, 1, keepdims=True))
     across = lax.rsqrt(diag_row)
     scale = jnp.where(row == col, jnp.broadcast_to(down, (n, n)), 0.0)
-    work = eliminate(jnp.concatenate([gram * down * across, scale], 1), 8)
+    work = jnp.concatenate([gram * down * across, scale], 1)
+    top = eliminate(work[: n // 2], 8, 0)
+    pivots = jnp.sum(jnp.where((row == col)[: n // 2], top[:, :n], 0.0), 1, keepdims=True)
+    h, m, l = split((top * (1.0 / pivots)).T[n // 2 : n], 3)
+    th, tm, tl = split(top, 3)
+    share = jnp.dot(
+        jnp.concatenate([h, h, m, h, m, l], 1),
+        jnp.concatenate([th, tm, th, tl, tm, th], 0),
+        preferred_element_type=jnp.float32,
+    )
+    low = eliminate(work[n // 2 :] - share, 8, n // 2)
+    work = jnp.concatenate([top, low], 0)
     upper = work[:, :n]
     left = lax.rsqrt(jnp.sum(jnp.where(row == col, upper, 0.0), 1, keepdims=True))
     return jnp.where(col >= row, upper * left * (diag_row * across), 0.0), work[:, n:] * left
 
 
-def pre(core_ref, slab_hbm, sketch_hbm, sketch_t_ref, slab_ref, give_ref, sketch_ref, arrived):
-    columns = slab_ref.shape[1]
-    chunks = arrived.shape[1]
-    width = columns // chunks
-    views = [pl.ds(i * width, width) for i in range(chunks)]
+def pre(widths, core_ref, slab_hbm, sketch_hbm, sketch_t_ref, slab_ref, give_ref, sketch_ref, arrived):
+    views, at = [], 0
+    for width in widths:
+        views.append(pl.ds(at, width))
+        at += width
     copies = [
         [
             pltpu.make_async_copy(source.at[:, view], target.at[:, view], arrived.at[j, i])
@@ -172,13 +193,14 @@
 LIMIT = pltpu.CompilerParams(vmem_limit_bytes=16 << 20)
 
 
-def begin(core, slab, sketch_matrix, chunks=4):
+def begin(core, slab, sketch_matrix):
     rows, columns = slab.shape
+    widths = [columns * part // 16 for part in (1, 3, 5, 7)]
     rank = sketch_matrix.shape[0]
     slab, sketch_matrix = (pltpu.with_memory_space_constraint(a, pltpu.HBM) for a in (slab, sketch_matrix))
     hbm = pl.BlockSpec(memory_space=pltpu.HBM)
     return pl.pallas_call(
-        pre,
+        functools.partial(pre, widths),
         out_shape=(
             pltpu.VMEM((rank, rows), jnp.float32),
             pltpu.VMEM(slab.shape, slab.dtype),
@@ -188,7 +210,7 @@
         out_specs=[VMEM] * 3,
         scratch_shapes=[
             pltpu.VMEM(sketch_matrix.shape, sketch_matrix.dtype),
-            pltpu.SemaphoreType.DMA((2, chunks)),
+            pltpu.SemaphoreType.DMA((2, len(widths))),
         ],
         compiler_params=LIMIT,
         name="sketch_and_cross_to_give",
@@ -214,9 +236,10 @@
     half = source.shape[0] * 128
     cross = jnp.concatenate([source[b] for b in range(source.shape[0])], 1)
     high, mid, low = split(cross, 3)
-    stack[...] = jnp.concatenate([high, mid, low, high], 0)
+    stack[...] = jnp.concatenate([high, mid], 0)
     view = pl.ds(pl.multiple_of(which * half, half), half)
-    out = lax.dot_general(stack[: 3 * rank], sketch_ref[:, view], LAST, preferred_element_type=jnp.float32)
+    three = jnp.concatenate([high, mid, low], 0)
+    out = lax.dot_general(three, sketch_ref[:, view], LAST, preferred_element_type=jnp.float32)
     return out[:rank] + (out[rank : 2 * rank] + out[2 * rank :])
 
 
@@ -229,7 +252,7 @@
     return pl.pallas_call(
         post_mine,
         out_shape=(
-            pltpu.VMEM((4 * rank, columns // 2), jnp.bfloat16),
+            pltpu.VMEM((2 * rank, columns // 2), jnp.bfloat16),
             pltpu.VMEM((rank, rank), jnp.float32),
         ),
         in_specs=[SCALAR, VMEM, VMEM],
@@ -252,15 +275,19 @@
     upper, inverse = factor(0.5 * (folded + folded.T))
     tri_ref[...] = upper * (1.0 / root)
     high, low = split(inverse, 2)
-    left = jnp.concatenate([high, high, high, low], 1)
+    left = jnp.concatenate(
+        [jnp.concatenate([high, high], 1), jnp.concatenate([low, jnp.zeros_like(low)], 1)], 0
+    )
     total = jnp.zeros((2 * rank, rank), jnp.float32)
     for which, stack in ((core, mine_stack), (1 - core, other_stack)):
-        part = jnp.dot(left, stack[...], preferred_element_type=jnp.float32)
-        proj_ref[:, pl.ds(pl.multiple_of(which * half, half), half)] = part
-        pair = split(part, 2)
-        total += lax.dot_general(
-            jnp.concatenate(pair, 0), pair[0], LAST, preferred_element_type=jnp.float32
-        )
+        for at in range(0, half, 512):
+            part = jnp.dot(left, stack[:, at : at + 512], preferred_element_type=jnp.float32)
+            part = part[:rank] + part[rank:]
+            proj_ref[:, pl.ds(pl.multiple_of(which * half + at, 128), 512)] = part
+            pair = split(part, 2)
+            total += lax.dot_general(
+                jnp.concatenate(pair, 0), pair[0], LAST, preferred_element_type=jnp.float32
+            )
     gram_ref[...] = (total[:rank] + (total[rank:] + total[rank:].T)) * (1.0 / columns)
     high, low = split(inverse * root, 2)
     left = jnp.concatenate([high, high, low], 1)
@@ -281,7 +308,7 @@
         ),
         in_specs=[SCALAR] + [VMEM] * 5,
         out_specs=[VMEM] * 4,
-        scratch_shapes=[pltpu.VMEM((4 * rank, columns // 2), jnp.bfloat16)],
+        scratch_shapes=[pltpu.VMEM((2 * rank, columns // 2), jnp.bfloat16)],
         compiler_params=pltpu.CompilerParams(vmem_limit_bytes=24 << 20),
         name="factor_and_project",
     )(core, mine_stack, folded, other, sketch_matrix, sketch_t)

time: 78.7 us -> 78.3 us (level)
  no operation moved by 1% of the time
where the time goes in v6:
time: 78.3 us; the launch traced here: 78 us
  blocking collectives  51.6 us (66%)
  starting transfers between devices  15 us (19%)
  Pallas kernels  8.14 us (10%)
  waiting for transfers between devices  2.32 us (3%)
    all_to_all x3, blocking collectives, exchange(): lax.all_to_all(pieces, 'rows', 0, 0, axis_index_groups=peers, tiled=True)  51.6 us
    ppermute x1, starting transfers between devices, shards(): got = lax.ppermute(give, 'rows', PAIRS)  8.79 us
    ppermute x1, starting transfers between devices, shards(): other = lax.ppermute(mine, 'rows', PAIRS)  6.23 us
    pallas_call x1, Pallas kernels, finish(): pl.pallas_call(functools.partial(post, root), out_shape=(jax.ShapeDtypeSt...  4.64 us
    pallas_call x1, Pallas kernels, begin(): pl.pallas_call(functools.partial(pre, widths), out_shape=(pltpu.VMEM((ran...  2.82 us
  transfers between devices with their start and end apart: 2, of which 2 were waited for; matrix products, arithmetic and copies ran while one was open for 0% of the time, Pallas kernels for 1%

profile of v6, /device:TPU:1, one launch (start us, length us, event | category | flops | bytes accessed | tf_op | source)
XLA Modules:
  0.0 78.0 jit_solution(1763296070251350392)
XLA Ops:
  0.6 2.8 %sketch_and_cross_to_give.1 = (f32[64,256]{1,0:T(8,128)S(1)}, bf16[256,4096]{1,0:T(8,128)(2,1)S(1)}, f32[16,64,128]{2,1,0:T(8,128)S(1)}) custom-call(s32[1]{0:T(128)} %bitcast.core_ref, bf16[256,4096]{1,0:T(8,128)(2,1)} %slab_hbm.1, bf16[64,4096]{1,0:T(8,128)(2,1)} %sketch_ref.3), custom_call_target="tpu_custom_call" | custom-call | tf_op jit(solution)/shard_map/sketch_and_cross_to_give/pallas_call | solution.py:202
  3.5 8.8 %collective-permute-start = (f32[16,64,128]{2,1,0:T(8,128)S(1)}, f32[16,64,128]{2,1,0:T(8,128)S(1)}, u32[]{:S(2)}, u32[]{:S(2)}) collective-permute-start(f32[16,64,128]{2,1,0:T(8,128)S(1)} %get-tuple-element.11), channel_id=1, source_target_pairs={{0,1},{1,0},{2,3},{3,2},{4,5},{5,4},{6,7},{7,6},{8,9},{9,8},{10,11... | collective-permute-start | bytes 1572872 | tf_op jit(solution)/shard_map/ppermute | solution.py:322
  12.3 0.3 cross_to_keep.1
  12.6 1.2 %collective-permute-done = f32[16,64,128]{2,1,0:T(8,128)S(1)} collective-permute-done((f32[16,64,128]{2,1,0:T(8,128)S(1)}, f32[16,64,128]{2,1,0:T(8,128)S(1)}, u32[]{:S(2)}, u32[]{:S(2)}) %collective-permute-start) | collective-permute-done | bytes 524320 | tf_op jit(solution)/shard_map/ppermute | solution.py:322
  13.8 0.1 add.8
  13.8 0.0 copy-start
  13.9 20.1 %all_to_all.15 = f32[128,8,128]{2,1,0:T(8,128)S(1)} all-to-all(f32[128,8,128]{2,1,0:T(8,128)S(1)} %bitcast.9), channel_id=1, replica_groups={{0,2,4,6,8,10,12,14,16,18,20,22,24,26,28,30,32,34,36,38,40,42,44,46,48,..., dimensions={0} | all-to-all | bytes 1048576 | tf_op jit(solution)/shard_map/all_to_all | solution.py:37
  34.0 14.5 %all_to_all.16 = f32[32,8,128]{2,1,0:T(8,128)S(1)} all-to-all(f32[32,8,128]{2,1,0:T(8,128)S(1)} %bitcast.13), channel_id=1, replica_groups={{0,64,128,192,256,320,384,448},{1,9,17,25,33,41,49,57},{2,66,130,194,25..., dimensions={0} | all-to-all | bytes 262144 | tf_op jit(solution)/shard_map/all_to_all | solution.py:37
  48.6 0.1 tile.20
  48.7 16.9 %all_to_all.17 = f32[128,8,128]{2,1,0:T(8,128)S(1)} all-to-all(f32[128,8,128]{2,1,0:T(8,128)S(1)} %bitcast.11), channel_id=1, replica_groups={{0,2,4,6,8,10,12,14,16,18,20,22,24,26,28,30,32,34,36,38,40,42,44,46,48,..., dimensions={0} | all-to-all | bytes 1048576 | tf_op jit(solution)/shard_map/all_to_all | solution.py:37
  65.6 6.2 %collective-permute-start.1 = (f32[16,64,128]{2,1,0:T(8,128)S(1)}, f32[16,64,128]{2,1,0:T(8,128)S(1)}, u32[]{:S(2)}, u32[]{:S(2)}) collective-permute-start(f32[16,64,128]{2,1,0:T(8,128)S(1)} %bitcast.7), channel_id=1, source_target_pairs={{0,1},{1,0},{2,3},{3,2},{4,5},{5,4},{6,7},{7,6},{8,9},{9,8},{10,11... | collective-permute-start | bytes 1572872 | tf_op jit(solution)/shard_map/ppermute | solution.py:325
  71.8 0.0 copy-done
  71.8 0.4 fold_mine.1
  72.2 1.1 %collective-permute-done.1.other_ref = f32[16,64,128]{2,1,0:T(8,128)S(1)} collective-permute-done((f32[16,64,128]{2,1,0:T(8,128)S(1)}, f32[16,64,128]{2,1,0:T(8,128)S(1)}, u32[]{:S(2)}, u32[]{:S(2)}) %collective-permute-start.1) | collective-permute-done | bytes 524320 | tf_op jit(solution)/shard_map/ppermute | solution.py:325
  73.3 4.6 %factor_and_project.1 = (bf16[64,256]{1,0:T(8,128)(2,1)}, f32[64,4096]{1,0:T(8,128)}, f32[64,64]{1,0:T(8,128)}, f32[64,64]{1,0:T(8,128)}) custom-call(s32[1]{0:T(128)} %bitcast.core_ref, bf16[128,2048]{1,0:T(8,128)(2,1)S(1)} %get-tuple-element.12.mine_stack, f32[64,64]{1,0:T(8,128)S(1)} %get-tuple-element.13.folded_ref, ...), custom_call_target="tpu_custom_call" | custom-call | tf_op jit(solution)/shard_map/factor_and_project/pallas_call | solution.py:301
  (3 shorter events, 0.1 us)
Async XLA Ops:
  3.5 10.3 %collective-permute-start = (f32[16,64,128]{2,1,0:T(8,128)S(1)}, f32[16,64,128]{2,1,0:T(8,128)S(1)}, u32[]{:S(2)}, u32[]{:S(2)}) collective-permute-start(f32[16,64,128]{2,1,0:T(8,128)S(1)} %get-tuple-element.11), channel_id=1, source_target_pairs={{0,1},{1,0},{2,3},{3,2},{4,5},{5,4},{6,7},{7,6},{8,9},{9,8},{10,11... | collective-permute-start | bytes 1572872 | tf_op jit(solution)/shard_map/ppermute | solution.py:322
  13.8 58.0 %copy-start = (bf16[64,4096]{1,0:T(8,128)(2,1)S(1)}, bf16[64,4096]{1,0:T(8,128)(2,1)}, u32[]{:S(2)}) copy-start(bf16[64,4096]{1,0:T(8,128)(2,1)} %sketch_ref.3) | copy-start | bytes 1572868
  65.6 7.8 %collective-permute-start.1 = (f32[16,64,128]{2,1,0:T(8,128)S(1)}, f32[16,64,128]{2,1,0:T(8,128)S(1)}, u32[]{:S(2)}, u32[]{:S(2)}) collective-permute-start(f32[16,64,128]{2,1,0:T(8,128)S(1)} %bitcast.7), channel_id=1, source_target_pairs={{0,1},{1,0},{2,3},{3,2},{4,5},{5,4},{6,7},{7,6},{8,9},{9,8},{10,11... | collective-permute-start | bytes 1572872 | tf_op jit(solution)/shard_map/ppermute | solution.py:325

commit v7 on v6

--- a/solution.py
+++ b/solution.py
@@ -62,65 +62,42 @@
     return out
 
 
-def eliminate(work, size, base):
+def eliminate(work, base):
     sub = lax.broadcasted_iota(jnp.int32, (8, 128), 0)
 
     def row(tile, k):
         return jnp.broadcast_to(tile[k : k + 1, :], (8, 128))
 
     work = [work[8 * b : 8 * b + 8] for b in range(work.shape[0] // 8)]
-    for first in range(0, 8 * len(work), size):
-        top, at = divmod(first, 8)
-        live = range(top, len(work))
+    for top in range(len(work)):
+        below = range(top + 1, len(work))
+        at = base + 8 * top
         column = [
-            {b: jnp.broadcast_to(work[b][:, base + first + k : base + first + k + 1], (8, 128)) for b in live}
-            for k in range(size)
+            {b: jnp.broadcast_to(work[b][:, at + k : at + k + 1], (8, 128)) for b in range(top, len(work))}
+            for k in range(8)
         ]
-        pivot = [row(work[top], at + k) for k in range(size)]
-        m = {(i, k): row(column[k][top], at + i) for k in range(size) for i in range(k, size)}
-        x, done, scaled = {}, {}, {}
-        for k in range(0, size, 2):
-            a, b, d = m[k, k], m[k + 1, k], m[k + 1, k + 1]
-            if k % 4 == 0:
-                det = a * d - b * b
-                y = {i: (d * m[i, k] - b * m[i, k + 1], a * m[i, k + 1] - b * m[i, k]) for i in (k + 2, k + 3)}
-                e, f, g = (
-                    det * m[i, j] - (y[i][0] * m[j, k] + y[i][1] * m[j, k + 1])
-                    for i, j in ((k + 2, k + 2), (k + 3, k + 2), (k + 3, k + 3))
-                )
-                after = det * (1.0 / (e * g - f * f))
-                inverse = 1.0 / det
-                ai, bi, di = a * inverse, b * inverse, d * inverse
-            else:
-                ai, bi, di = e * after, f * after, g * after
-            rest = range(k + 2, size)
-            for i in rest:
-                x[i, k] = di * m[i, k] - bi * m[i, k + 1]
-                x[i, k + 1] = ai * m[i, k + 1] - bi * m[i, k]
-            for i in rest:
-                for j in range(k + 2, i + 1):
-                    m[i, j] = m[i, j] - x[i, k] * m[j, k] - x[i, k + 1] * m[j, k + 1]
-            done[k] = pivot[k]
-            done[k + 1] = pivot[k + 1] - (b * (1.0 / a)) * pivot[k]
-            scaled[k] = di * pivot[k] - bi * pivot[k + 1]
-            scaled[k + 1] = ai * pivot[k + 1] - bi * pivot[k]
-            for i in rest:
-                pivot[i] = pivot[i] - x[i, k] * pivot[k] - x[i, k + 1] * pivot[k + 1]
-        for k in reversed(range(size)):
-            for i in range(k // 2 * 2 + 2, size):
-                scaled[k] = scaled[k] - x[i, k] * scaled[i]
-        for b in live:
-            new = work[b]
-            if b > top or at + size < 8:
-                terms = [column[k][b] * scaled[k] for k in range(size)]
-                while len(terms) > 1:
-                    terms = [terms[i] + terms[i + 1] for i in range(0, len(terms), 2)]
-                new = new - terms[0]
-            if b == top:
-                new = jnp.where(sub >= at + size, new, work[b])
-                for k in range(1, size):
-                    new = jnp.where(sub == at + k, done[k], new)
-            work[b] = new
+        pivot = [row(work[top], k) for k in range(8)]
+        m = {(i, k): row(column[k][top], i) for k in range(8) for i in range(k, 8)}
+        scaled = []
+        for k in range(8):
+            inverse = 1.0 / m[k, k]
+            scaled.append(pivot[k] * inverse)
+            x = {i: m[i, k] * inverse for i in range(k + 1, 8)}
+            for i in x:
+                for j in range(k + 1, i + 1):
+                    m[i, j] = m[i, j] - x[i] * m[j, k]
+                pivot[i] = pivot[i] - x[i] * pivot[k]
+                for b in below:
+                    column[i][b] = column[i][b] - x[i] * column[k][b]
+        for b in below:
+            terms = [column[k][b] * scaled[k] for k in range(8)]
+            while len(terms) > 1:
+                terms = [terms[i] + terms[i + 1] for i in range(0, len(terms), 2)]
+            work[b] = work[b] - terms[0]
+        done = pivot[0]
+        for k in range(1, 8):
+            done = jnp.where(sub == k, pivot[k], done)
+        work[top] = done
     return jnp.concatenate(work, 0)
 
 
@@ -134,17 +111,7 @@
     across = lax.rsqrt(diag_row)
     scale = jnp.where(row == col, jnp.broadcast_to(down, (n, n)), 0.0)
     work = jnp.concatenate([gram * down * across, scale], 1)
-    top = eliminate(work[: n // 2], 8, 0)
-    pivots = jnp.sum(jnp.where((row == col)[: n // 2], top[:, :n], 0.0), 1, keepdims=True)
-    h, m, l = split((top * (1.0 / pivots)).T[n // 2 : n], 3)
-    th, tm, tl = split(top, 3)
-    share = jnp.dot(
-        jnp.concatenate([h, h, m, h, m, l], 1),
-        jnp.concatenate([th, tm, th, tl, tm, th], 0),
-        preferred_element_type=jnp.float32,
-    )
-    low = eliminate(work[n // 2 :] - share, 8, n // 2)
-    work = jnp.concatenate([top, low], 0)
+    work = eliminate(work, 0)
     upper = work[:, :n]
     left = lax.rsqrt(jnp.sum(jnp.where(row == col, upper, 0.0), 1, keepdims=True))
     return jnp.where(col >= row, upper * left * (diag_row * across), 0.0), work[:, n:] * left
@@ -231,15 +198,25 @@
     )(core, sketch_t, slab)
 
 
+def right_parts(value):
+    high, mid, low = split(value, 3)
+    return jnp.concatenate([high, mid, low, high], 0)
+
+
+def left_parts(value):
+    high, mid, low = split(value, 3)
+    zero = jnp.zeros_like(high)
+    rows = ((high, high, high, low), (mid, mid, zero, zero))
+    return jnp.concatenate([jnp.concatenate(parts, 1) for parts in rows], 0)
+
+
 def fold_half(which, source, sketch_ref, stack):
     rank = sketch_ref.shape[0]
     half = source.shape[0] * 128
     cross = jnp.concatenate([source[b] for b in range(source.shape[0])], 1)
-    high, mid, low = split(cross, 3)
-    stack[...] = jnp.concatenate([high, mid], 0)
+    stack[...] = right_parts(cross)
     view = pl.ds(pl.multiple_of(which * half, half), half)
-    three = jnp.concatenate([high, mid, low], 0)
-    out = lax.dot_general(three, sketch_ref[:, view], LAST, preferred_element_type=jnp.float32)
+    out = lax.dot_general(stack[: 3 * rank], sketch_ref[:, view], LAST, preferred_element_type=jnp.float32)
     return out[:rank] + (out[rank : 2 * rank] + out[2 * rank :])
 
 
@@ -252,7 +229,7 @@
     return pl.pallas_call(
         post_mine,
         out_shape=(
-            pltpu.VMEM((2 * rank, columns // 2), jnp.bfloat16),
+            pltpu.VMEM((4 * rank, columns // 2), jnp.bfloat16),
             pltpu.VMEM((rank, rank), jnp.float32),
         ),
         in_specs=[SCALAR, VMEM, VMEM],
@@ -274,10 +251,7 @@
     folded = folded_ref[...] + fold_half(1 - core, other_ref, sketch_ref, other_stack)
     upper, inverse = factor(0.5 * (folded + folded.T))
     tri_ref[...] = upper * (1.0 / root)
-    high, low = split(inverse, 2)
-    left = jnp.concatenate(
-        [jnp.concatenate([high, high], 1), jnp.concatenate([low, jnp.zeros_like(low)], 1)], 0
-    )
+    left = left_parts(inverse)
     total = jnp.zeros((2 * rank, rank), jnp.float32)
     for which, stack in ((core, mine_stack), (1 - core, other_stack)):
         for at in range(0, half, 512):
@@ -289,11 +263,8 @@
                 jnp.concatenate(pair, 0), pair[0], LAST, preferred_element_type=jnp.float32
             )
     gram_ref[...] = (total[:rank] + (total[rank:] + total[rank:].T)) * (1.0 / columns)
-    high, low = split(inverse * root, 2)
-    left = jnp.concatenate([high, high, low], 1)
-    s_high, s_low = split(sketch_t_ref[...], 2)
-    right = jnp.concatenate([s_high, s_low, s_high], 0)
-    q_ref[...] = jnp.dot(left, right, preferred_element_type=jnp.float32).astype(q_ref.dtype)
+    part = jnp.dot(left_parts(inverse * root), right_parts(sketch_t_ref[...]), preferred_element_type=jnp.float32)
+    q_ref[...] = (part[:rank] + part[rank:]).astype(q_ref.dtype)
 
 
 def finish(core, mine_stack, folded, other, sketch_matrix, sketch_t, root):
@@ -308,7 +279,7 @@
         ),
         in_specs=[SCALAR] + [VMEM] * 5,
         out_specs=[VMEM] * 4,
-        scratch_shapes=[pltpu.VMEM((2 * rank, columns // 2), jnp.bfloat16)],
+        scratch_shapes=[pltpu.VMEM((4 * rank, columns // 2), jnp.bfloat16)],
         compiler_params=pltpu.CompilerParams(vmem_limit_bytes=24 << 20),
         name="factor_and_project",
     )(core, mine_stack, folded, other, sketch_matrix, sketch_t)

time: 78.3 us -> 78.2 us (level)
  no operation moved by 1% of the time
where the time goes in v7:
time: 78.2 us; the launch traced here: 77.9 us
  blocking collectives  51.6 us (66%)
  starting transfers between devices  15 us (19%)
  Pallas kernels  8.12 us (10%)
  waiting for transfers between devices  2.29 us (3%)
    all_to_all x3, blocking collectives, exchange(): lax.all_to_all(pieces, 'rows', 0, 0, axis_index_groups=peers, tiled=True)  51.6 us
    ppermute x1, starting transfers between devices, shards(): got = lax.ppermute(give, 'rows', PAIRS)  8.79 us
    ppermute x1, starting transfers between devices, shards(): other = lax.ppermute(mine, 'rows', PAIRS)  6.23 us
    pallas_call x1, Pallas kernels, finish(): pl.pallas_call(functools.partial(post, root), out_shape=(jax.ShapeDtypeSt...  4.57 us
    pallas_call x1, Pallas kernels, begin(): pl.pallas_call(functools.partial(pre, widths), out_shape=(pltpu.VMEM((ran...  2.82 us
  transfers between devices with their start and end apart: 2, of which 2 were waited for; matrix products, arithmetic and copies ran while one was open for 0% of the time, Pallas kernels for 1%

profile of v7, /device:TPU:1, one launch (start us, length us, event | category | flops | bytes accessed | tf_op | source)
XLA Modules:
  0.0 77.9 jit_solution(15405166099575222661)
XLA Ops:
  0.6 2.8 %sketch_and_cross_to_give.1 = (f32[64,256]{1,0:T(8,128)S(1)}, bf16[256,4096]{1,0:T(8,128)(2,1)S(1)}, f32[16,64,128]{2,1,0:T(8,128)S(1)}) custom-call(s32[1]{0:T(128)} %bitcast.core_ref, bf16[256,4096]{1,0:T(8,128)(2,1)} %slab_hbm.1, bf16[64,4096]{1,0:T(8,128)(2,1)} %sketch_ref.3), custom_call_target="tpu_custom_call" | custom-call | tf_op jit(solution)/shard_map/sketch_and_cross_to_give/pallas_call | solution.py:169
  3.5 8.8 %collective-permute-start = (f32[16,64,128]{2,1,0:T(8,128)S(1)}, f32[16,64,128]{2,1,0:T(8,128)S(1)}, u32[]{:S(2)}, u32[]{:S(2)}) collective-permute-start(f32[16,64,128]{2,1,0:T(8,128)S(1)} %get-tuple-element.11), channel_id=1, source_target_pairs={{0,1},{1,0},{2,3},{3,2},{4,5},{5,4},{6,7},{7,6},{8,9},{9,8},{10,11... | collective-permute-start | bytes 1572872 | tf_op jit(solution)/shard_map/ppermute | solution.py:293
  12.3 0.3 cross_to_keep.1
  12.6 1.2 %collective-permute-done = f32[16,64,128]{2,1,0:T(8,128)S(1)} collective-permute-done((f32[16,64,128]{2,1,0:T(8,128)S(1)}, f32[16,64,128]{2,1,0:T(8,128)S(1)}, u32[]{:S(2)}, u32[]{:S(2)}) %collective-permute-start) | collective-permute-done | bytes 524320 | tf_op jit(solution)/shard_map/ppermute | solution.py:293
  13.8 0.1 add.8
  13.8 0.0 copy-start
  13.9 20.1 %all_to_all.15 = f32[128,8,128]{2,1,0:T(8,128)S(1)} all-to-all(f32[128,8,128]{2,1,0:T(8,128)S(1)} %bitcast.9), channel_id=1, replica_groups={{0,2,4,6,8,10,12,14,16,18,20,22,24,26,28,30,32,34,36,38,40,42,44,46,48,..., dimensions={0} | all-to-all | bytes 1048576 | tf_op jit(solution)/shard_map/all_to_all | solution.py:37
  34.0 14.5 %all_to_all.16 = f32[32,8,128]{2,1,0:T(8,128)S(1)} all-to-all(f32[32,8,128]{2,1,0:T(8,128)S(1)} %bitcast.13), channel_id=1, replica_groups={{0,64,128,192,256,320,384,448},{1,9,17,25,33,41,49,57},{2,66,130,194,25..., dimensions={0} | all-to-all | bytes 262144 | tf_op jit(solution)/shard_map/all_to_all | solution.py:37
  48.6 0.1 tile.20
  48.7 16.9 %all_to_all.17 = f32[128,8,128]{2,1,0:T(8,128)S(1)} all-to-all(f32[128,8,128]{2,1,0:T(8,128)S(1)} %bitcast.11), channel_id=1, replica_groups={{0,2,4,6,8,10,12,14,16,18,20,22,24,26,28,30,32,34,36,38,40,42,44,46,48,..., dimensions={0} | all-to-all | bytes 1048576 | tf_op jit(solution)/shard_map/all_to_all | solution.py:37
  65.6 6.2 %collective-permute-start.1 = (f32[16,64,128]{2,1,0:T(8,128)S(1)}, f32[16,64,128]{2,1,0:T(8,128)S(1)}, u32[]{:S(2)}, u32[]{:S(2)}) collective-permute-start(f32[16,64,128]{2,1,0:T(8,128)S(1)} %bitcast.7), channel_id=1, source_target_pairs={{0,1},{1,0},{2,3},{3,2},{4,5},{5,4},{6,7},{7,6},{8,9},{9,8},{10,11... | collective-permute-start | bytes 1572872 | tf_op jit(solution)/shard_map/ppermute | solution.py:296
  71.8 0.0 copy-done
  71.8 0.4 fold_mine.1
  72.2 1.1 %collective-permute-done.1.other_ref = f32[16,64,128]{2,1,0:T(8,128)S(1)} collective-permute-done((f32[16,64,128]{2,1,0:T(8,128)S(1)}, f32[16,64,128]{2,1,0:T(8,128)S(1)}, u32[]{:S(2)}, u32[]{:S(2)}) %collective-permute-start.1) | collective-permute-done | bytes 524320 | tf_op jit(solution)/shard_map/ppermute | solution.py:296
  73.3 4.6 %factor_and_project.1 = (bf16[64,256]{1,0:T(8,128)(2,1)}, f32[64,4096]{1,0:T(8,128)}, f32[64,64]{1,0:T(8,128)}, f32[64,64]{1,0:T(8,128)}) custom-call(s32[1]{0:T(128)} %bitcast.core_ref, bf16[256,2048]{1,0:T(8,128)(2,1)S(1)} %get-tuple-element.12.mine_stack, f32[64,64]{1,0:T(8,128)S(1)} %get-tuple-element.13.folded_ref, ...), custom_call_target="tpu_custom_call" | custom-call | tf_op jit(solution)/shard_map/factor_and_project/pallas_call | solution.py:272
  (3 shorter events, 0.1 us)
Async XLA Ops:
  3.5 10.3 %collective-permute-start = (f32[16,64,128]{2,1,0:T(8,128)S(1)}, f32[16,64,128]{2,1,0:T(8,128)S(1)}, u32[]{:S(2)}, u32[]{:S(2)}) collective-permute-start(f32[16,64,128]{2,1,0:T(8,128)S(1)} %get-tuple-element.11), channel_id=1, source_target_pairs={{0,1},{1,0},{2,3},{3,2},{4,5},{5,4},{6,7},{7,6},{8,9},{9,8},{10,11... | collective-permute-start | bytes 1572872 | tf_op jit(solution)/shard_map/ppermute | solution.py:293
  13.8 58.0 %copy-start = (bf16[64,4096]{1,0:T(8,128)(2,1)S(1)}, bf16[64,4096]{1,0:T(8,128)(2,1)}, u32[]{:S(2)}) copy-start(bf16[64,4096]{1,0:T(8,128)(2,1)} %sketch_ref.3) | copy-start | bytes 1572868
  65.6 7.8 %collective-permute-start.1 = (f32[16,64,128]{2,1,0:T(8,128)S(1)}, f32[16,64,128]{2,1,0:T(8,128)S(1)}, u32[]{:S(2)}, u32[]{:S(2)}) collective-permute-start(f32[16,64,128]{2,1,0:T(8,128)S(1)} %bitcast.7), channel_id=1, source_target_pairs={{0,1},{1,0},{2,3},{3,2},{4,5},{5,4},{6,7},{7,6},{8,9},{9,8},{10,11... | collective-permute-start | bytes 1572872 | tf_op jit(solution)/shard_map/ppermute | solution.py:296

commit v8 on v7

--- a/solution.py
+++ b/solution.py
@@ -28,8 +28,8 @@
     return list(out.values())
 
 
-PLANE = groups(("yx", "zx"))
-LINE = groups(("z", "y"))
+PLANE = groups(("zx", "yx"))
+LINE = groups(("y", "z"))
 PAIRS = [(i, i ^ 1) for i in range(math.prod(SIZES.values()))]
 
 

time: 78.2 us -> 78.2 us (level)
  no operation moved by 1% of the time
where the time goes in v8:
time: 78.2 us; the launch traced here: 77.9 us
  blocking collectives  51.6 us (66%)
  starting transfers between devices  15 us (19%)
  Pallas kernels  8.12 us (10%)
  waiting for transfers between devices  2.29 us (3%)
    all_to_all x3, blocking collectives, exchange(): lax.all_to_all(pieces, 'rows', 0, 0, axis_index_groups=peers, tiled=True)  51.6 us
    ppermute x1, starting transfers between devices, shards(): got = lax.ppermute(give, 'rows', PAIRS)  8.79 us
    ppermute x1, starting transfers between devices, shards(): other = lax.ppermute(mine, 'rows', PAIRS)  6.23 us
    pallas_call x1, Pallas kernels, finish(): pl.pallas_call(functools.partial(post, root), out_shape=(jax.ShapeDtypeSt...  4.57 us
    pallas_call x1, Pallas kernels, begin(): pl.pallas_call(functools.partial(pre, widths), out_shape=(pltpu.VMEM((ran...  2.82 us
  transfers between devices with their start and end apart: 2, of which 2 were waited for; matrix products, arithmetic and copies ran while one was open for 0% of the time, Pallas kernels for 1%

profile of v8, /device:TPU:1, one launch (start us, length us, event | category | flops | bytes accessed | tf_op | source)
XLA Modules:
  0.0 77.9 jit_solution(8619681921647152993)
XLA Ops:
  0.6 2.8 %sketch_and_cross_to_give.1 = (f32[64,256]{1,0:T(8,128)S(1)}, bf16[256,4096]{1,0:T(8,128)(2,1)S(1)}, f32[16,64,128]{2,1,0:T(8,128)S(1)}) custom-call(s32[1]{0:T(128)} %bitcast.core_ref, bf16[256,4096]{1,0:T(8,128)(2,1)} %slab_hbm.1, bf16[64,4096]{1,0:T(8,128)(2,1)} %sketch_ref.3), custom_call_target="tpu_custom_call" | custom-call | tf_op jit(solution)/shard_map/sketch_and_cross_to_give/pallas_call | solution.py:169
  3.5 8.8 %collective-permute-start = (f32[16,64,128]{2,1,0:T(8,128)S(1)}, f32[16,64,128]{2,1,0:T(8,128)S(1)}, u32[]{:S(2)}, u32[]{:S(2)}) collective-permute-start(f32[16,64,128]{2,1,0:T(8,128)S(1)} %get-tuple-element.11), channel_id=1, source_target_pairs={{0,1},{1,0},{2,3},{3,2},{4,5},{5,4},{6,7},{7,6},{8,9},{9,8},{10,11... | collective-permute-start | bytes 1572872 | tf_op jit(solution)/shard_map/ppermute | solution.py:293
  12.3 0.3 cross_to_keep.1
  12.6 1.2 %collective-permute-done = f32[16,64,128]{2,1,0:T(8,128)S(1)} collective-permute-done((f32[16,64,128]{2,1,0:T(8,128)S(1)}, f32[16,64,128]{2,1,0:T(8,128)S(1)}, u32[]{:S(2)}, u32[]{:S(2)}) %collective-permute-start) | collective-permute-done | bytes 524320 | tf_op jit(solution)/shard_map/ppermute | solution.py:293
  13.8 0.1 add.8
  13.8 0.0 copy-start
  13.9 17.0 %all_to_all.15 = f32[128,8,128]{2,1,0:T(8,128)S(1)} all-to-all(f32[128,8,128]{2,1,0:T(8,128)S(1)} %bitcast.9), channel_id=1, replica_groups={{0,2,4,6,64,66,68,70,128,130,132,134,192,194,196,198,256,258,260,262,32..., dimensions={0} | all-to-all | bytes 1048576 | tf_op jit(solution)/shard_map/all_to_all | solution.py:37
  31.0 17.6 %all_to_all.16 = f32[32,8,128]{2,1,0:T(8,128)S(1)} all-to-all(f32[32,8,128]{2,1,0:T(8,128)S(1)} %bitcast.13), channel_id=1, replica_groups={{0,8,16,24,32,40,48,56},{1,65,129,193,257,321,385,449},{2,10,18,26,34,4..., dimensions={0} | all-to-all | bytes 262144 | tf_op jit(solution)/shard_map/all_to_all | solution.py:37
  48.6 0.1 tile.20
  48.7 16.9 %all_to_all.17 = f32[128,8,128]{2,1,0:T(8,128)S(1)} all-to-all(f32[128,8,128]{2,1,0:T(8,128)S(1)} %bitcast.11), channel_id=1, replica_groups={{0,2,4,6,64,66,68,70,128,130,132,134,192,194,196,198,256,258,260,262,32..., dimensions={0} | all-to-all | bytes 1048576 | tf_op jit(solution)/shard_map/all_to_all | solution.py:37
  65.6 6.2 %collective-permute-start.1 = (f32[16,64,128]{2,1,0:T(8,128)S(1)}, f32[16,64,128]{2,1,0:T(8,128)S(1)}, u32[]{:S(2)}, u32[]{:S(2)}) collective-permute-start(f32[16,64,128]{2,1,0:T(8,128)S(1)} %bitcast.7), channel_id=1, source_target_pairs={{0,1},{1,0},{2,3},{3,2},{4,5},{5,4},{6,7},{7,6},{8,9},{9,8},{10,11... | collective-permute-start | bytes 1572872 | tf_op jit(solution)/shard_map/ppermute | solution.py:296
  71.8 0.0 copy-done
  71.8 0.4 fold_mine.1
  72.2 1.1 %collective-permute-done.1.other_ref = f32[16,64,128]{2,1,0:T(8,128)S(1)} collective-permute-done((f32[16,64,128]{2,1,0:T(8,128)S(1)}, f32[16,64,128]{2,1,0:T(8,128)S(1)}, u32[]{:S(2)}, u32[]{:S(2)}) %collective-permute-start.1) | collective-permute-done | bytes 524320 | tf_op jit(solution)/shard_map/ppermute | solution.py:296
  73.3 4.6 %factor_and_project.1 = (bf16[64,256]{1,0:T(8,128)(2,1)}, f32[64,4096]{1,0:T(8,128)}, f32[64,64]{1,0:T(8,128)}, f32[64,64]{1,0:T(8,128)}) custom-call(s32[1]{0:T(128)} %bitcast.core_ref, bf16[256,2048]{1,0:T(8,128)(2,1)S(1)} %get-tuple-element.12.mine_stack, f32[64,64]{1,0:T(8,128)S(1)} %get-tuple-element.13.folded_ref, ...), custom_call_target="tpu_custom_call" | custom-call | tf_op jit(solution)/shard_map/factor_and_project/pallas_call | solution.py:272
  (3 shorter events, 0.1 us)
Async XLA Ops:
  3.5 10.3 %collective-permute-start = (f32[16,64,128]{2,1,0:T(8,128)S(1)}, f32[16,64,128]{2,1,0:T(8,128)S(1)}, u32[]{:S(2)}, u32[]{:S(2)}) collective-permute-start(f32[16,64,128]{2,1,0:T(8,128)S(1)} %get-tuple-element.11), channel_id=1, source_target_pairs={{0,1},{1,0},{2,3},{3,2},{4,5},{5,4},{6,7},{7,6},{8,9},{9,8},{10,11... | collective-permute-start | bytes 1572872 | tf_op jit(solution)/shard_map/ppermute | solution.py:293
  13.8 58.0 %copy-start = (bf16[64,4096]{1,0:T(8,128)(2,1)S(1)}, bf16[64,4096]{1,0:T(8,128)(2,1)}, u32[]{:S(2)}) copy-start(bf16[64,4096]{1,0:T(8,128)(2,1)} %sketch_ref.3) | copy-start | bytes 1572868
  65.6 7.8 %collective-permute-start.1 = (f32[16,64,128]{2,1,0:T(8,128)S(1)}, f32[16,64,128]{2,1,0:T(8,128)S(1)}, u32[]{:S(2)}, u32[]{:S(2)}) collective-permute-start(f32[16,64,128]{2,1,0:T(8,128)S(1)} %bitcast.7), channel_id=1, source_target_pairs={{0,1},{1,0},{2,3},{3,2},{4,5},{5,4},{6,7},{7,6},{8,9},{9,8},{10,11... | collective-permute-start | bytes 1572872 | tf_op jit(solution)/shard_map/ppermute | solution.py:296

commit v9 on v7

--- a/solution.py
+++ b/solution.py
@@ -37,18 +37,33 @@
     return lax.all_to_all(pieces, "rows", 0, 0, axis_index_groups=peers, tiled=True)
 
 
-def summed(tiles, count):
-    return tiles.reshape(count, tiles.shape[0] // count, 8, 128).sum(0)
-
-
-def spread(tiles, peers):
-    return exchange(jnp.tile(tiles, (len(peers[0]), 1, 1)), peers)
+def total_kernel(size, got_ref, out_ref):
+    senders, receivers = got_ref.shape[0] // size, out_ref.shape[0] // size
+    for t in range(size):
+        terms = [got_ref[k * size + t] for k in range(senders)]
+        while len(terms) > 1:
+            terms = [terms[i] + terms[i + 1] for i in range(0, len(terms), 2)]
+        for k in range(receivers):
+            out_ref[k * size + t] = terms[0]
+
+
+def total(got, size, receivers):
+    vmem = pl.BlockSpec(memory_space=pltpu.VMEM)
+    return pl.pallas_call(
+        functools.partial(total_kernel, size),
+        out_shape=pltpu.VMEM((size * receivers, 8, 128), jnp.float32),
+        in_specs=[vmem],
+        out_specs=vmem,
+        compiler_params=pltpu.CompilerParams(vmem_limit_bytes=16 << 20),
+        name="sum_and_repeat",
+    )(got)
 
 
 def all_reduce(part):
-    part = summed(exchange(part, PLANE), len(PLANE[0]))
-    part = summed(spread(part, LINE), len(LINE[0]))
-    return spread(part, PLANE)
+    plane, line = len(PLANE[0]), len(LINE[0])
+    size = part.shape[0] // plane
+    got = exchange(total(exchange(part, PLANE), size, line), LINE)
+    return exchange(total(got, size, plane), PLANE)
 
 
 LAST = (((1,), (1,)), ((), ()))
@@ -62,42 +77,52 @@
     return out
 
 
-def eliminate(work, base):
+def eliminate(work, base, size=16):
     sub = lax.broadcasted_iota(jnp.int32, (8, 128), 0)
 
     def row(tile, k):
         return jnp.broadcast_to(tile[k : k + 1, :], (8, 128))
 
     work = [work[8 * b : 8 * b + 8] for b in range(work.shape[0] // 8)]
-    for top in range(len(work)):
-        below = range(top + 1, len(work))
-        at = base + 8 * top
+    for first in range(0, 8 * len(work), size):
+        top, off = divmod(first, 8)
+        tops = range(top, (first + size + 7) // 8)
+        ends_inside = (first + size) % 8 != 0
+        below = range(tops[-1] if ends_inside else tops[-1] + 1, len(work))
+        at = base + first
         column = [
             {b: jnp.broadcast_to(work[b][:, at + k : at + k + 1], (8, 128)) for b in range(top, len(work))}
-            for k in range(8)
+            for k in range(size)
         ]
-        pivot = [row(work[top], k) for k in range(8)]
-        m = {(i, k): row(column[k][top], i) for k in range(8) for i in range(k, 8)}
+        pivot = [row(work[(first + k) // 8], (first + k) % 8) for k in range(size)]
+        m = {(i, k): row(column[k][(first + i) // 8], (first + i) % 8) for k in range(size) for i in range(k, size)}
         scaled = []
-        for k in range(8):
+        for k in range(size):
             inverse = 1.0 / m[k, k]
             scaled.append(pivot[k] * inverse)
-            x = {i: m[i, k] * inverse for i in range(k + 1, 8)}
+            x = {i: m[i, k] * inverse for i in range(k + 1, size)}
             for i in x:
                 for j in range(k + 1, i + 1):
                     m[i, j] = m[i, j] - x[i] * m[j, k]
                 pivot[i] = pivot[i] - x[i] * pivot[k]
                 for b in below:
                     column[i][b] = column[i][b] - x[i] * column[k][b]
+        new = {}
         for b in below:
-            terms = [column[k][b] * scaled[k] for k in range(8)]
+            terms = [column[k][b] * scaled[k] for k in range(size)]
             while len(terms) > 1:
                 terms = [terms[i] + terms[i + 1] for i in range(0, len(terms), 2)]
-            work[b] = work[b] - terms[0]
-        done = pivot[0]
-        for k in range(1, 8):
-            done = jnp.where(sub == k, pivot[k], done)
-        work[top] = done
+            new[b] = work[b] - terms[0]
+        for b in tops:
+            done = new.get(b, work[b])
+            if ends_inside or off:
+                done = jnp.where(sub >= off + size, done, work[b])
+            for k in range(size):
+                if (first + k) // 8 == b:
+                    done = jnp.where(sub == (first + k) % 8, pivot[k], done)
+            new[b] = done
+        for b in new:
+            work[b] = new[b]
     return jnp.concatenate(work, 0)
 
 

time: 78.2 us -> 78.1 us (level)
  no operation moved by 1% of the time
where the time goes in v9:
time: 78.1 us; the launch traced here: 77.8 us
  blocking collectives  51.6 us (66%)
  starting transfers between devices  15 us (19%)
  Pallas kernels  8.17 us (10%)
  waiting for transfers between devices  2.29 us (3%)
    all_to_all x3, blocking collectives, exchange(): lax.all_to_all(pieces, 'rows', 0, 0, axis_index_groups=peers, tiled=True)  51.6 us
    ppermute x1, starting transfers between devices, shards(): got = lax.ppermute(give, 'rows', PAIRS)  8.79 us
    ppermute x1, starting transfers between devices, shards(): other = lax.ppermute(mine, 'rows', PAIRS)  6.23 us
    pallas_call x1, Pallas kernels, finish(): pl.pallas_call(functools.partial(post, root), out_shape=(jax.ShapeDtypeSt...  4.53 us
    pallas_call x1, Pallas kernels, begin(): pl.pallas_call(functools.partial(pre, widths), out_shape=(pltpu.VMEM((ran...  2.82 us
  transfers between devices with their start and end apart: 2, of which 2 were waited for; matrix products, arithmetic and copies ran while one was open for 0% of the time, Pallas kernels for 1%

profile of v9, /device:TPU:1, one launch (start us, length us, event | category | flops | bytes accessed | tf_op | source)
XLA Modules:
  0.0 77.8 jit_solution(15743151638370523853)
XLA Ops:
  0.6 2.8 %sketch_and_cross_to_give.1 = (f32[64,256]{1,0:T(8,128)S(1)}, bf16[256,4096]{1,0:T(8,128)(2,1)S(1)}, f32[16,64,128]{2,1,0:T(8,128)S(1)}) custom-call(s32[1]{0:T(128)} %bitcast.core_ref, bf16[256,4096]{1,0:T(8,128)(2,1)} %slab_hbm.1, bf16[64,4096]{1,0:T(8,128)(2,1)} %sketch_ref.3), custom_call_target="tpu_custom_call" | custom-call | tf_op jit(solution)/shard_map/sketch_and_cross_to_give/pallas_call | solution.py:194
  3.5 8.8 %collective-permute-start = (f32[16,64,128]{2,1,0:T(8,128)S(1)}, f32[16,64,128]{2,1,0:T(8,128)S(1)}, u32[]{:S(2)}, u32[]{:S(2)}) collective-permute-start(f32[16,64,128]{2,1,0:T(8,128)S(1)} %get-tuple-element.11), channel_id=1, source_target_pairs={{0,1},{1,0},{2,3},{3,2},{4,5},{5,4},{6,7},{7,6},{8,9},{9,8},{10,11... | collective-permute-start | bytes 1572872 | tf_op jit(solution)/shard_map/ppermute | solution.py:318
  12.3 0.3 cross_to_keep.1
  12.6 1.2 %collective-permute-done = f32[16,64,128]{2,1,0:T(8,128)S(1)} collective-permute-done((f32[16,64,128]{2,1,0:T(8,128)S(1)}, f32[16,64,128]{2,1,0:T(8,128)S(1)}, u32[]{:S(2)}, u32[]{:S(2)}) %collective-permute-start) | collective-permute-done | bytes 524320 | tf_op jit(solution)/shard_map/ppermute | solution.py:318
  13.8 0.1 add.8
  13.8 0.0 copy-start
  13.9 20.1 %all_to_all.15.got_ref = f32[128,8,128]{2,1,0:T(8,128)S(1)} all-to-all(f32[128,8,128]{2,1,0:T(8,128)S(1)} %bitcast.5), channel_id=1, replica_groups={{0,2,4,6,8,10,12,14,16,18,20,22,24,26,28,30,32,34,36,38,40,42,44,46,48,..., dimensions={0} | all-to-all | bytes 1048576 | tf_op jit(solution)/shard_map/all_to_all | solution.py:37
  34.0 14.5 %all_to_all.16.got_ref = f32[32,8,128]{2,1,0:T(8,128)S(1)} all-to-all(f32[32,8,128]{2,1,0:T(8,128)S(1)} %sum_and_repeat.2), channel_id=1, replica_groups={{0,64,128,192,256,320,384,448},{1,9,17,25,33,41,49,57},{2,66,130,194,25..., dimensions={0} | all-to-all | bytes 262144 | tf_op jit(solution)/shard_map/all_to_all | solution.py:37
  48.6 0.1 sum_and_repeat.3
  48.6 16.9 %all_to_all.17 = f32[128,8,128]{2,1,0:T(8,128)S(1)} all-to-all(f32[128,8,128]{2,1,0:T(8,128)S(1)} %sum_and_repeat.3), channel_id=1, replica_groups={{0,2,4,6,8,10,12,14,16,18,20,22,24,26,28,30,32,34,36,38,40,42,44,46,48,..., dimensions={0} | all-to-all | bytes 1048576 | tf_op jit(solution)/shard_map/all_to_all | solution.py:37
  65.5 6.2 %collective-permute-start.1 = (f32[16,64,128]{2,1,0:T(8,128)S(1)}, f32[16,64,128]{2,1,0:T(8,128)S(1)}, u32[]{:S(2)}, u32[]{:S(2)}) collective-permute-start(f32[16,64,128]{2,1,0:T(8,128)S(1)} %bitcast.3), channel_id=1, source_target_pairs={{0,1},{1,0},{2,3},{3,2},{4,5},{5,4},{6,7},{7,6},{8,9},{9,8},{10,11... | collective-permute-start | bytes 1572872 | tf_op jit(solution)/shard_map/ppermute | solution.py:321
  71.8 0.0 copy-done
  71.8 0.4 fold_mine.1
  72.2 1.1 %collective-permute-done.1.other_ref = f32[16,64,128]{2,1,0:T(8,128)S(1)} collective-permute-done((f32[16,64,128]{2,1,0:T(8,128)S(1)}, f32[16,64,128]{2,1,0:T(8,128)S(1)}, u32[]{:S(2)}, u32[]{:S(2)}) %collective-permute-start.1) | collective-permute-done | bytes 524320 | tf_op jit(solution)/shard_map/ppermute | solution.py:321
  73.3 4.5 %factor_and_project.1 = (bf16[64,256]{1,0:T(8,128)(2,1)}, f32[64,4096]{1,0:T(8,128)}, f32[64,64]{1,0:T(8,128)}, f32[64,64]{1,0:T(8,128)}) custom-call(s32[1]{0:T(128)} %bitcast.core_ref, bf16[256,2048]{1,0:T(8,128)(2,1)S(1)} %get-tuple-element.12.mine_stack, f32[64,64]{1,0:T(8,128)S(1)} %get-tuple-element.13.folded_ref, ...), custom_call_target="tpu_custom_call" | custom-call | tf_op jit(solution)/shard_map/factor_and_project/pallas_call | solution.py:297
  (1 shorter events, 0.0 us)
Async XLA Ops:
  3.5 10.3 %collective-permute-start = (f32[16,64,128]{2,1,0:T(8,128)S(1)}, f32[16,64,128]{2,1,0:T(8,128)S(1)}, u32[]{:S(2)}, u32[]{:S(2)}) collective-permute-start(f32[16,64,128]{2,1,0:T(8,128)S(1)} %get-tuple-element.11), channel_id=1, source_target_pairs={{0,1},{1,0},{2,3},{3,2},{4,5},{5,4},{6,7},{7,6},{8,9},{9,8},{10,11... | collective-permute-start | bytes 1572872 | tf_op jit(solution)/shard_map/ppermute | solution.py:318
  13.8 57.9 %copy-start = (bf16[64,4096]{1,0:T(8,128)(2,1)S(1)}, bf16[64,4096]{1,0:T(8,128)(2,1)}, u32[]{:S(2)}) copy-start(bf16[64,4096]{1,0:T(8,128)(2,1)} %sketch_ref.3) | copy-start | bytes 1572868
  65.5 7.8 %collective-permute-start.1 = (f32[16,64,128]{2,1,0:T(8,128)S(1)}, f32[16,64,128]{2,1,0:T(8,128)S(1)}, u32[]{:S(2)}, u32[]{:S(2)}) collective-permute-start(f32[16,64,128]{2,1,0:T(8,128)S(1)} %bitcast.3), channel_id=1, source_target_pairs={{0,1},{1,0},{2,3},{3,2},{4,5},{5,4},{6,7},{7,6},{8,9},{9,8},{10,11... | collective-permute-start | bytes 1572872 | tf_op jit(solution)/shard_map/ppermute | solution.py:321

commit v10 on v8

--- a/solution.py
+++ b/solution.py
@@ -18,18 +18,15 @@
     return coords
 
 
-def groups(axes_of_core):
+def groups(held):
     out = {}
     for index in range(math.prod(SIZES.values())):
-        coords = place(index)
-        axes = axes_of_core[coords["c"]]
-        key = (coords["c"],) + tuple(value for name, value in coords.items() if name not in axes)
-        out.setdefault(key, []).append(index)
+        out.setdefault(held(**place(index)), []).append(index)
     return list(out.values())
 
 
-PLANE = groups(("zx", "yx"))
-LINE = groups(("y", "z"))
+NEAR = groups(lambda x, y, z, c: (c, y // 2, z // 2))
+FAR = groups(lambda x, y, z, c: (c, x, y % 2, z % 2))
 PAIRS = [(i, i ^ 1) for i in range(math.prod(SIZES.values()))]
 
 
@@ -46,9 +43,9 @@
 
 
 def all_reduce(part):
-    part = summed(exchange(part, PLANE), len(PLANE[0]))
-    part = summed(spread(part, LINE), len(LINE[0]))
-    return spread(part, PLANE)
+    part = summed(exchange(part, NEAR), len(NEAR[0]))
+    part = summed(spread(part, FAR), len(FAR[0]))
+    return spread(part, NEAR)
 
 
 LAST = (((1,), (1,)), ((), ()))

time: 78.2 us -> 82.2 us (1.051)
  blocking collectives: 51.6 us -> 57.8 us
  starting transfers between devices: 15 us -> 12.8 us
    all_to_all x3, blocking collectives: 51.6 us -> 57.8 us  [exchange(): lax.all_to_all(pieces, 'rows', 0, 0, axis_index_groups=peers, tiled=True)]
    ppermute x1, starting transfers between devices: 6.23 us -> 3.99 us  [shards(): other = lax.ppermute(mine, 'rows', PAIRS)]
where the time goes in v10:
time: 82.2 us; the launch traced here: 81.9 us
  blocking collectives  57.8 us (70%)
  starting transfers between devices  12.8 us (16%)
  Pallas kernels  8.12 us (10%)
  waiting for transfers between devices  2.29 us (3%)
    all_to_all x3, blocking collectives, exchange(): lax.all_to_all(pieces, 'rows', 0, 0, axis_index_groups=peers, tiled=True)  57.8 us
    ppermute x1, starting transfers between devices, shards(): got = lax.ppermute(give, 'rows', PAIRS)  8.79 us
    pallas_call x1, Pallas kernels, finish(): pl.pallas_call(functools.partial(post, root), out_shape=(jax.ShapeDtypeSt...  4.57 us
    ppermute x1, starting transfers between devices, shards(): other = lax.ppermute(mine, 'rows', PAIRS)  3.99 us
    pallas_call x1, Pallas kernels, begin(): pl.pallas_call(functools.partial(pre, widths), out_shape=(pltpu.VMEM((ran...  2.82 us
  transfers between devices with their start and end apart: 2, of which 2 were waited for; matrix products, arithmetic and copies ran while one was open for 0% of the time, Pallas kernels for 1%

profile of v10, /device:TPU:1, one launch (start us, length us, event | category | flops | bytes accessed | tf_op | source)
XLA Modules:
  0.0 81.9 jit_solution(8376760603052369995)
XLA Ops:
  0.6 2.8 %sketch_and_cross_to_give.1 = (f32[64,256]{1,0:T(8,128)S(1)}, bf16[256,4096]{1,0:T(8,128)(2,1)S(1)}, f32[16,64,128]{2,1,0:T(8,128)S(1)}) custom-call(s32[1]{0:T(128)} %bitcast.core_ref, bf16[256,4096]{1,0:T(8,128)(2,1)} %slab_hbm.1, bf16[64,4096]{1,0:T(8,128)(2,1)} %sketch_ref.3), custom_call_target="tpu_custom_call" | custom-call | tf_op jit(solution)/shard_map/sketch_and_cross_to_give/pallas_call | solution.py:166
  3.5 8.8 %collective-permute-start = (f32[16,64,128]{2,1,0:T(8,128)S(1)}, f32[16,64,128]{2,1,0:T(8,128)S(1)}, u32[]{:S(2)}, u32[]{:S(2)}) collective-permute-start(f32[16,64,128]{2,1,0:T(8,128)S(1)} %get-tuple-element.11), channel_id=1, source_target_pairs={{0,1},{1,0},{2,3},{3,2},{4,5},{5,4},{6,7},{7,6},{8,9},{9,8},{10,11... | collective-permute-start | bytes 1572872 | tf_op jit(solution)/shard_map/ppermute | solution.py:290
  12.3 0.3 cross_to_keep.1
  12.6 1.2 %collective-permute-done = f32[16,64,128]{2,1,0:T(8,128)S(1)} collective-permute-done((f32[16,64,128]{2,1,0:T(8,128)S(1)}, f32[16,64,128]{2,1,0:T(8,128)S(1)}, u32[]{:S(2)}, u32[]{:S(2)}) %collective-permute-start) | collective-permute-done | bytes 524320 | tf_op jit(solution)/shard_map/ppermute | solution.py:290
  13.8 0.1 add.8
  13.8 13.3 %all_to_all.15 = f32[128,8,128]{2,1,0:T(8,128)S(1)} all-to-all(f32[128,8,128]{2,1,0:T(8,128)S(1)} %bitcast.9), channel_id=1, replica_groups={{0,2,4,6,8,10,12,14,64,66,68,70,72,74,76,78},{1,3,5,7,9,11,13,15,65,67,..., dimensions={0} | all-to-all | bytes 1048576 | tf_op jit(solution)/shard_map/all_to_all | solution.py:34
  27.1 0.0 copy-start
  27.2 30.6 %all_to_all.16 = f32[128,8,128]{2,1,0:T(8,128)S(1)} all-to-all(f32[128,8,128]{2,1,0:T(8,128)S(1)} %bitcast.12), channel_id=1, replica_groups={{0,16,32,48,128,144,160,176,256,272,288,304,384,400,416,432},{1,17,33,4..., dimensions={0} | all-to-all | bytes 1048576 | tf_op jit(solution)/shard_map/all_to_all | solution.py:34
  57.9 14.0 %all_to_all.17 = f32[128,8,128]{2,1,0:T(8,128)S(1)} all-to-all(f32[128,8,128]{2,1,0:T(8,128)S(1)} %bitcast.13), channel_id=1, replica_groups={{0,2,4,6,8,10,12,14,64,66,68,70,72,74,76,78},{1,3,5,7,9,11,13,15,65,67,..., dimensions={0} | all-to-all | bytes 1048576 | tf_op jit(solution)/shard_map/all_to_all | solution.py:34
  71.9 4.0 %collective-permute-start.1 = (f32[16,64,128]{2,1,0:T(8,128)S(1)}, f32[16,64,128]{2,1,0:T(8,128)S(1)}, u32[]{:S(2)}, u32[]{:S(2)}) collective-permute-start(f32[16,64,128]{2,1,0:T(8,128)S(1)} %bitcast.7), channel_id=1, source_target_pairs={{0,1},{1,0},{2,3},{3,2},{4,5},{5,4},{6,7},{7,6},{8,9},{9,8},{10,11... | collective-permute-start | bytes 1572872 | tf_op jit(solution)/shard_map/ppermute | solution.py:293
  75.9 0.0 copy-done
  75.9 0.4 fold_mine.1
  76.3 1.1 %collective-permute-done.1.other_ref = f32[16,64,128]{2,1,0:T(8,128)S(1)} collective-permute-done((f32[16,64,128]{2,1,0:T(8,128)S(1)}, f32[16,64,128]{2,1,0:T(8,128)S(1)}, u32[]{:S(2)}, u32[]{:S(2)}) %collective-permute-start.1) | collective-permute-done | bytes 524320 | tf_op jit(solution)/shard_map/ppermute | solution.py:293
  77.4 4.6 %factor_and_project.1 = (bf16[64,256]{1,0:T(8,128)(2,1)}, f32[64,4096]{1,0:T(8,128)}, f32[64,64]{1,0:T(8,128)}, f32[64,64]{1,0:T(8,128)}) custom-call(s32[1]{0:T(128)} %bitcast.core_ref, bf16[256,2048]{1,0:T(8,128)(2,1)S(1)} %get-tuple-element.12.mine_stack, f32[64,64]{1,0:T(8,128)S(1)} %get-tuple-element.13.folded_ref, ...), custom_call_target="tpu_custom_call" | custom-call | tf_op jit(solution)/shard_map/factor_and_project/pallas_call | solution.py:269
  (4 shorter events, 0.2 us)
Async XLA Ops:
  3.5 10.3 %collective-permute-start = (f32[16,64,128]{2,1,0:T(8,128)S(1)}, f32[16,64,128]{2,1,0:T(8,128)S(1)}, u32[]{:S(2)}, u32[]{:S(2)}) collective-permute-start(f32[16,64,128]{2,1,0:T(8,128)S(1)} %get-tuple-element.11), channel_id=1, source_target_pairs={{0,1},{1,0},{2,3},{3,2},{4,5},{5,4},{6,7},{7,6},{8,9},{9,8},{10,11... | collective-permute-start | bytes 1572872 | tf_op jit(solution)/shard_map/ppermute | solution.py:290
  27.1 48.7 %copy-start = (bf16[64,4096]{1,0:T(8,128)(2,1)S(1)}, bf16[64,4096]{1,0:T(8,128)(2,1)}, u32[]{:S(2)}) copy-start(bf16[64,4096]{1,0:T(8,128)(2,1)} %sketch_ref.3) | copy-start | bytes 1572868
  71.9 5.5 %collective-permute-start.1 = (f32[16,64,128]{2,1,0:T(8,128)S(1)}, f32[16,64,128]{2,1,0:T(8,128)S(1)}, u32[]{:S(2)}, u32[]{:S(2)}) collective-permute-start(f32[16,64,128]{2,1,0:T(8,128)S(1)} %bitcast.7), channel_id=1, source_target_pairs={{0,1},{1,0},{2,3},{3,2},{4,5},{5,4},{6,7},{7,6},{8,9},{9,8},{10,11... | collective-permute-start | bytes 1572872 | tf_op jit(solution)/shard_map/ppermute | solution.py:293

commit v11 on v9

--- a/solution.py
+++ b/solution.py
@@ -37,33 +37,18 @@
     return lax.all_to_all(pieces, "rows", 0, 0, axis_index_groups=peers, tiled=True)
 
 
-def total_kernel(size, got_ref, out_ref):
-    senders, receivers = got_ref.shape[0] // size, out_ref.shape[0] // size
-    for t in range(size):
-        terms = [got_ref[k * size + t] for k in range(senders)]
-        while len(terms) > 1:
-            terms = [terms[i] + terms[i + 1] for i in range(0, len(terms), 2)]
-        for k in range(receivers):
-            out_ref[k * size + t] = terms[0]
-
-
-def total(got, size, receivers):
-    vmem = pl.BlockSpec(memory_space=pltpu.VMEM)
-    return pl.pallas_call(
-        functools.partial(total_kernel, size),
-        out_shape=pltpu.VMEM((size * receivers, 8, 128), jnp.float32),
-        in_specs=[vmem],
-        out_specs=vmem,
-        compiler_params=pltpu.CompilerParams(vmem_limit_bytes=16 << 20),
-        name="sum_and_repeat",
-    )(got)
+def summed(tiles, count):
+    return tiles.reshape(count, tiles.shape[0] // count, 8, 128).sum(0)
+
+
+def spread(tiles, peers):
+    return exchange(jnp.tile(tiles, (len(peers[0]), 1, 1)), peers)
 
 
 def all_reduce(part):
-    plane, line = len(PLANE[0]), len(LINE[0])
-    size = part.shape[0] // plane
-    got = exchange(total(exchange(part, PLANE), size, line), LINE)
-    return exchange(total(got, size, plane), PLANE)
+    part = summed(exchange(part, PLANE), len(PLANE[0]))
+    part = summed(spread(part, LINE), len(LINE[0]))
+    return spread(part, PLANE)
 
 
 LAST = (((1,), (1,)), ((), ()))

time: 78.1 us -> 78.1 us (level)
  no operation moved by 1% of the time
where the time goes in v11:
time: 78.1 us; the launch traced here: 77.8 us
  blocking collectives  51.6 us (66%)
  starting transfers between devices  15 us (19%)
  Pallas kernels  8.08 us (10%)
  waiting for transfers between devices  2.29 us (3%)
    all_to_all x3, blocking collectives, exchange(): lax.all_to_all(pieces, 'rows', 0, 0, axis_index_groups=peers, tiled=True)  51.6 us
    ppermute x1, starting transfers between devices, shards(): got = lax.ppermute(give, 'rows', PAIRS)  8.79 us
    ppermute x1, starting transfers between devices, shards(): other = lax.ppermute(mine, 'rows', PAIRS)  6.23 us
    pallas_call x1, Pallas kernels, finish(): pl.pallas_call(functools.partial(post, root), out_shape=(jax.ShapeDtypeSt...  4.54 us
    pallas_call x1, Pallas kernels, begin(): pl.pallas_call(functools.partial(pre, widths), out_shape=(pltpu.VMEM((ran...  2.82 us
  transfers between devices with their start and end apart: 2, of which 2 were waited for; matrix products, arithmetic and copies ran while one was open for 0% of the time, Pallas kernels for 1%

profile of v11, /device:TPU:1, one launch (start us, length us, event | category | flops | bytes accessed | tf_op | source)
XLA Modules:
  0.0 77.8 jit_solution(730017020718856799)
XLA Ops:
  0.6 2.8 %sketch_and_cross_to_give.1 = (f32[64,256]{1,0:T(8,128)S(1)}, bf16[256,4096]{1,0:T(8,128)(2,1)S(1)}, f32[16,64,128]{2,1,0:T(8,128)S(1)}) custom-call(s32[1]{0:T(128)} %bitcast.core_ref, bf16[256,4096]{1,0:T(8,128)(2,1)} %slab_hbm.1, bf16[64,4096]{1,0:T(8,128)(2,1)} %sketch_ref.3), custom_call_target="tpu_custom_call" | custom-call | tf_op jit(solution)/shard_map/sketch_and_cross_to_give/pallas_call | solution.py:179
  3.5 8.8 %collective-permute-start = (f32[16,64,128]{2,1,0:T(8,128)S(1)}, f32[16,64,128]{2,1,0:T(8,128)S(1)}, u32[]{:S(2)}, u32[]{:S(2)}) collective-permute-start(f32[16,64,128]{2,1,0:T(8,128)S(1)} %get-tuple-element.11), channel_id=1, source_target_pairs={{0,1},{1,0},{2,3},{3,2},{4,5},{5,4},{6,7},{7,6},{8,9},{9,8},{10,11... | collective-permute-start | bytes 1572872 | tf_op jit(solution)/shard_map/ppermute | solution.py:303
  12.3 0.3 cross_to_keep.1
  12.6 1.2 %collective-permute-done = f32[16,64,128]{2,1,0:T(8,128)S(1)} collective-permute-done((f32[16,64,128]{2,1,0:T(8,128)S(1)}, f32[16,64,128]{2,1,0:T(8,128)S(1)}, u32[]{:S(2)}, u32[]{:S(2)}) %collective-permute-start) | collective-permute-done | bytes 524320 | tf_op jit(solution)/shard_map/ppermute | solution.py:303
  13.8 0.1 add.8
  13.8 0.0 copy-start
  13.9 20.1 %all_to_all.15 = f32[128,8,128]{2,1,0:T(8,128)S(1)} all-to-all(f32[128,8,128]{2,1,0:T(8,128)S(1)} %bitcast.9), channel_id=1, replica_groups={{0,2,4,6,8,10,12,14,16,18,20,22,24,26,28,30,32,34,36,38,40,42,44,46,48,..., dimensions={0} | all-to-all | bytes 1048576 | tf_op jit(solution)/shard_map/all_to_all | solution.py:37
  34.0 14.5 %all_to_all.16 = f32[32,8,128]{2,1,0:T(8,128)S(1)} all-to-all(f32[32,8,128]{2,1,0:T(8,128)S(1)} %bitcast.13), channel_id=1, replica_groups={{0,64,128,192,256,320,384,448},{1,9,17,25,33,41,49,57},{2,66,130,194,25..., dimensions={0} | all-to-all | bytes 262144 | tf_op jit(solution)/shard_map/all_to_all | solution.py:37
  48.6 0.1 tile.20
  48.7 16.9 %all_to_all.17 = f32[128,8,128]{2,1,0:T(8,128)S(1)} all-to-all(f32[128,8,128]{2,1,0:T(8,128)S(1)} %bitcast.11), channel_id=1, replica_groups={{0,2,4,6,8,10,12,14,16,18,20,22,24,26,28,30,32,34,36,38,40,42,44,46,48,..., dimensions={0} | all-to-all | bytes 1048576 | tf_op jit(solution)/shard_map/all_to_all | solution.py:37
  65.6 6.2 %collective-permute-start.1 = (f32[16,64,128]{2,1,0:T(8,128)S(1)}, f32[16,64,128]{2,1,0:T(8,128)S(1)}, u32[]{:S(2)}, u32[]{:S(2)}) collective-permute-start(f32[16,64,128]{2,1,0:T(8,128)S(1)} %bitcast.7), channel_id=1, source_target_pairs={{0,1},{1,0},{2,3},{3,2},{4,5},{5,4},{6,7},{7,6},{8,9},{9,8},{10,11... | collective-permute-start | bytes 1572872 | tf_op jit(solution)/shard_map/ppermute | solution.py:306
  71.8 0.0 copy-done
  71.8 0.4 fold_mine.1
  72.2 1.1 %collective-permute-done.1.other_ref = f32[16,64,128]{2,1,0:T(8,128)S(1)} collective-permute-done((f32[16,64,128]{2,1,0:T(8,128)S(1)}, f32[16,64,128]{2,1,0:T(8,128)S(1)}, u32[]{:S(2)}, u32[]{:S(2)}) %collective-permute-start.1) | collective-permute-done | bytes 524320 | tf_op jit(solution)/shard_map/ppermute | solution.py:306
  73.3 4.5 %factor_and_project.1 = (bf16[64,256]{1,0:T(8,128)(2,1)}, f32[64,4096]{1,0:T(8,128)}, f32[64,64]{1,0:T(8,128)}, f32[64,64]{1,0:T(8,128)}) custom-call(s32[1]{0:T(128)} %bitcast.core_ref, bf16[256,2048]{1,0:T(8,128)(2,1)S(1)} %get-tuple-element.12.mine_stack, f32[64,64]{1,0:T(8,128)S(1)} %get-tuple-element.13.folded_ref, ...), custom_call_target="tpu_custom_call" | custom-call | tf_op jit(solution)/shard_map/factor_and_project/pallas_call | solution.py:282
  (3 shorter events, 0.1 us)
Async XLA Ops:
  3.5 10.3 %collective-permute-start = (f32[16,64,128]{2,1,0:T(8,128)S(1)}, f32[16,64,128]{2,1,0:T(8,128)S(1)}, u32[]{:S(2)}, u32[]{:S(2)}) collective-permute-start(f32[16,64,128]{2,1,0:T(8,128)S(1)} %get-tuple-element.11), channel_id=1, source_target_pairs={{0,1},{1,0},{2,3},{3,2},{4,5},{5,4},{6,7},{7,6},{8,9},{9,8},{10,11... | collective-permute-start | bytes 1572872 | tf_op jit(solution)/shard_map/ppermute | solution.py:303
  13.8 58.0 %copy-start = (bf16[64,4096]{1,0:T(8,128)(2,1)S(1)}, bf16[64,4096]{1,0:T(8,128)(2,1)}, u32[]{:S(2)}) copy-start(bf16[64,4096]{1,0:T(8,128)(2,1)} %sketch_ref.3) | copy-start | bytes 1572868
  65.6 7.8 %collective-permute-start.1 = (f32[16,64,128]{2,1,0:T(8,128)S(1)}, f32[16,64,128]{2,1,0:T(8,128)S(1)}, u32[]{:S(2)}, u32[]{:S(2)}) collective-permute-start(f32[16,64,128]{2,1,0:T(8,128)S(1)} %bitcast.7), channel_id=1, source_target_pairs={{0,1},{1,0},{2,3},{3,2},{4,5},{5,4},{6,7},{7,6},{8,9},{9,8},{10,11... | collective-permute-start | bytes 1572872 | tf_op jit(solution)/shard_map/ppermute | solution.py:306

commit v12 on v11

--- a/solution.py
+++ b/solution.py
@@ -261,6 +261,8 @@
     folded = folded_ref[...] + fold_half(1 - core, other_ref, sketch_ref, other_stack)
     upper, inverse = factor(0.5 * (folded + folded.T))
     tri_ref[...] = upper * (1.0 / root)
+    part = jnp.dot(left_parts(inverse * root), right_parts(sketch_t_ref[...]), preferred_element_type=jnp.float32)
+    q_ref[...] = (part[:rank] + part[rank:]).astype(q_ref.dtype)
     left = left_parts(inverse)
     total = jnp.zeros((2 * rank, rank), jnp.float32)
     for which, stack in ((core, mine_stack), (1 - core, other_stack)):
@@ -273,8 +275,6 @@
                 jnp.concatenate(pair, 0), pair[0], LAST, preferred_element_type=jnp.float32
             )
     gram_ref[...] = (total[:rank] + (total[rank:] + total[rank:].T)) * (1.0 / columns)
-    part = jnp.dot(left_parts(inverse * root), right_parts(sketch_t_ref[...]), preferred_element_type=jnp.float32)
-    q_ref[...] = (part[:rank] + part[rank:]).astype(q_ref.dtype)
 
 
 def finish(core, mine_stack, folded, other, sketch_matrix, sketch_t, root):

time: 78.1 us -> 78.2 us (level)
  no operation moved by 1% of the time
where the time goes in v12:
time: 78.2 us; the launch traced here: 77.9 us
  blocking collectives  51.6 us (66%)
  starting transfers between devices  15 us (19%)
  Pallas kernels  8.11 us (10%)
  waiting for transfers between devices  2.29 us (3%)
    all_to_all x3, blocking collectives, exchange(): lax.all_to_all(pieces, 'rows', 0, 0, axis_index_groups=peers, tiled=True)  51.6 us
    ppermute x1, starting transfers between devices, shards(): got = lax.ppermute(give, 'rows', PAIRS)  8.79 us
    ppermute x1, starting transfers between devices, shards(): other = lax.ppermute(mine, 'rows', PAIRS)  6.23 us
    pallas_call x1, Pallas kernels, finish(): pl.pallas_call(functools.partial(post, root), out_shape=(jax.ShapeDtypeSt...  4.57 us
    pallas_call x1, Pallas kernels, begin(): pl.pallas_call(functools.partial(pre, widths), out_shape=(pltpu.VMEM((ran...  2.82 us
  transfers between devices with their start and end apart: 2, of which 2 were waited for; matrix products, arithmetic and copies ran while one was open for 0% of the time, Pallas kernels for 1%

profile of v12, /device:TPU:1, one launch (start us, length us, event | category | flops | bytes accessed | tf_op | source)
XLA Modules:
  0.0 77.9 jit_solution(286805829208962926)
XLA Ops:
  0.6 2.8 %sketch_and_cross_to_give.1 = (f32[64,256]{1,0:T(8,128)S(1)}, bf16[256,4096]{1,0:T(8,128)(2,1)S(1)}, f32[16,64,128]{2,1,0:T(8,128)S(1)}) custom-call(s32[1]{0:T(128)} %bitcast.core_ref, bf16[256,4096]{1,0:T(8,128)(2,1)} %slab_hbm.1, bf16[64,4096]{1,0:T(8,128)(2,1)} %sketch_ref.3), custom_call_target="tpu_custom_call" | custom-call | tf_op jit(solution)/shard_map/sketch_and_cross_to_give/pallas_call | solution.py:179
  3.5 8.8 %collective-permute-start = (f32[16,64,128]{2,1,0:T(8,128)S(1)}, f32[16,64,128]{2,1,0:T(8,128)S(1)}, u32[]{:S(2)}, u32[]{:S(2)}) collective-permute-start(f32[16,64,128]{2,1,0:T(8,128)S(1)} %get-tuple-element.11), channel_id=1, source_target_pairs={{0,1},{1,0},{2,3},{3,2},{4,5},{5,4},{6,7},{7,6},{8,9},{9,8},{10,11... | collective-permute-start | bytes 1572872 | tf_op jit(solution)/shard_map/ppermute | solution.py:303
  12.3 0.3 cross_to_keep.1
  12.6 1.2 %collective-permute-done = f32[16,64,128]{2,1,0:T(8,128)S(1)} collective-permute-done((f32[16,64,128]{2,1,0:T(8,128)S(1)}, f32[16,64,128]{2,1,0:T(8,128)S(1)}, u32[]{:S(2)}, u32[]{:S(2)}) %collective-permute-start) | collective-permute-done | bytes 524320 | tf_op jit(solution)/shard_map/ppermute | solution.py:303
  13.8 0.1 add.8
  13.8 0.0 copy-start
  13.9 20.1 %all_to_all.15 = f32[128,8,128]{2,1,0:T(8,128)S(1)} all-to-all(f32[128,8,128]{2,1,0:T(8,128)S(1)} %bitcast.9), channel_id=1, replica_groups={{0,2,4,6,8,10,12,14,16,18,20,22,24,26,28,30,32,34,36,38,40,42,44,46,48,..., dimensions={0} | all-to-all | bytes 1048576 | tf_op jit(solution)/shard_map/all_to_all | solution.py:37
  34.0 14.5 %all_to_all.16 = f32[32,8,128]{2,1,0:T(8,128)S(1)} all-to-all(f32[32,8,128]{2,1,0:T(8,128)S(1)} %bitcast.13), channel_id=1, replica_groups={{0,64,128,192,256,320,384,448},{1,9,17,25,33,41,49,57},{2,66,130,194,25..., dimensions={0} | all-to-all | bytes 262144 | tf_op jit(solution)/shard_map/all_to_all | solution.py:37
  48.6 0.1 tile.20
  48.7 16.9 %all_to_all.17 = f32[128,8,128]{2,1,0:T(8,128)S(1)} all-to-all(f32[128,8,128]{2,1,0:T(8,128)S(1)} %bitcast.11), channel_id=1, replica_groups={{0,2,4,6,8,10,12,14,16,18,20,22,24,26,28,30,32,34,36,38,40,42,44,46,48,..., dimensions={0} | all-to-all | bytes 1048576 | tf_op jit(solution)/shard_map/all_to_all | solution.py:37
  65.6 6.2 %collective-permute-start.1 = (f32[16,64,128]{2,1,0:T(8,128)S(1)}, f32[16,64,128]{2,1,0:T(8,128)S(1)}, u32[]{:S(2)}, u32[]{:S(2)}) collective-permute-start(f32[16,64,128]{2,1,0:T(8,128)S(1)} %bitcast.7), channel_id=1, source_target_pairs={{0,1},{1,0},{2,3},{3,2},{4,5},{5,4},{6,7},{7,6},{8,9},{9,8},{10,11... | collective-permute-start | bytes 1572872 | tf_op jit(solution)/shard_map/ppermute | solution.py:306
  71.8 0.0 copy-done
  71.8 0.4 fold_mine.1
  72.2 1.1 %collective-permute-done.1.other_ref = f32[16,64,128]{2,1,0:T(8,128)S(1)} collective-permute-done((f32[16,64,128]{2,1,0:T(8,128)S(1)}, f32[16,64,128]{2,1,0:T(8,128)S(1)}, u32[]{:S(2)}, u32[]{:S(2)}) %collective-permute-start.1) | collective-permute-done | bytes 524320 | tf_op jit(solution)/shard_map/ppermute | solution.py:306
  73.3 4.6 %factor_and_project.1 = (bf16[64,256]{1,0:T(8,128)(2,1)}, f32[64,4096]{1,0:T(8,128)}, f32[64,64]{1,0:T(8,128)}, f32[64,64]{1,0:T(8,128)}) custom-call(s32[1]{0:T(128)} %bitcast.core_ref, bf16[256,2048]{1,0:T(8,128)(2,1)S(1)} %get-tuple-element.12.mine_stack, f32[64,64]{1,0:T(8,128)S(1)} %get-tuple-element.13.folded_ref, ...), custom_call_target="tpu_custom_call" | custom-call | tf_op jit(solution)/shard_map/factor_and_project/pallas_call | solution.py:282
  (3 shorter events, 0.1 us)
Async XLA Ops:
  3.5 10.3 %collective-permute-start = (f32[16,64,128]{2,1,0:T(8,128)S(1)}, f32[16,64,128]{2,1,0:T(8,128)S(1)}, u32[]{:S(2)}, u32[]{:S(2)}) collective-permute-start(f32[16,64,128]{2,1,0:T(8,128)S(1)} %get-tuple-element.11), channel_id=1, source_target_pairs={{0,1},{1,0},{2,3},{3,2},{4,5},{5,4},{6,7},{7,6},{8,9},{9,8},{10,11... | collective-permute-start | bytes 1572872 | tf_op jit(solution)/shard_map/ppermute | solution.py:303
  13.8 58.0 %copy-start = (bf16[64,4096]{1,0:T(8,128)(2,1)S(1)}, bf16[64,4096]{1,0:T(8,128)(2,1)}, u32[]{:S(2)}) copy-start(bf16[64,4096]{1,0:T(8,128)(2,1)} %sketch_ref.3) | copy-start | bytes 1572868
  65.6 7.8 %collective-permute-start.1 = (f32[16,64,128]{2,1,0:T(8,128)S(1)}, f32[16,64,128]{2,1,0:T(8,128)S(1)}, u32[]{:S(2)}, u32[]{:S(2)}) collective-permute-start(f32[16,64,128]{2,1,0:T(8,128)S(1)} %bitcast.7), channel_id=1, source_target_pairs={{0,1},{1,0},{2,3},{3,2},{4,5},{5,4},{6,7},{7,6},{8,9},{9,8},{10,11... | collective-permute-start | bytes 1572872 | tf_op jit(solution)/shard_map/ppermute | solution.py:306
